TPU v7x, 32 devices: a whole 2x2x4 slice. The times are simulated.
32 devices in a mesh: dop: 8 (over z, x), rng: 4 (over y, core).
Axes of the slice: x: 2, y: 2, z: 4, core: 2. Of those that a mesh axis runs over, the one named last changes fastest.
Arguments:
- echoes: bfloat16 [2, 256, 64, 16384], P(None, 'dop', None, 'rng'), may hold values from -6 to 6
- chirp: bfloat16 [2, 512], replicated, may hold values from -0.1875 to 0.1875
- ridge: int32 [256], P('dop'), may hold values from 0 to 1, as said below
- counts: int32 [256], P('dop'), may hold values from 1 to 8
Outputs:
- whitened: bfloat16 [256, 128, 16384], P('dop', None, 'rng')
Inputs may be any that keep to these rules, and one draw needn't show every extreme that they name: `ridge`: exactly 64 bins are 1 and they are consecutive, cyclically over the 256 bins.
All inputs are finite; a program needn't handle non-finite values.
Results may differ from a plain program's by a relative error of at most 0.008.
Values may be sent and summed in bfloat16 or wider, within the bound.
No kernel may reach another device: no remote copies, remote signals or barrier semaphores. Data moves between devices by JAX's collectives and lax.ppermute only.
A program may use at most 256 MiB of HBM per device.

v0:
```python
import math

import jax
import jax.numpy as jnp
from jax import lax
from jax.sharding import PartitionSpec as P

TRAIN_BLK = 512


LOADING = 0.1


def shifted(block, axis, distance):
    devices = range(lax.axis_size(axis))
    route = [(i - distance, i) for i in devices if i - distance in devices]
    return lax.ppermute(block, axis, route)


def prefix_2(array, axis, combine, identity):
    size, here = (lax.axis_size(axis), lax.axis_index(axis))
    everything = lax.all_gather(array, axis)
    start = jnp.broadcast_to(jnp.asarray(identity, array.dtype), array.shape)

    def step(k, before):
        reached = k < here
        new = combine(before, everything[k])
        return jnp.where(reached, new, before)

    return lax.fori_loop(0, size, step, start)


def filter_table(chirp, tap_count):
    length = 3 * tap_count
    halves = []
    for component in range(2):
        sequence = jnp.concatenate([jnp.zeros((2 * tap_count,), chirp.dtype), chirp[component]])
        tiled = jnp.tile(sequence, 2 * tap_count)[: 2 * tap_count * (length - 1)]
        halves.append(tiled.reshape(2 * tap_count, length - 1)[:, :tap_count])
    real_table = halves[0]
    imag_table = halves[1]
    upper_rows = jnp.concatenate([real_table, imag_table], axis=1)
    lower_rows = jnp.concatenate([-imag_table, real_table], axis=1)
    return jnp.concatenate([upper_rows, lower_rows], axis=0)


def doppler_table(pulse_count):
    bin_index = jnp.arange(pulse_count, dtype=jnp.int32)
    product = bin_index[:, None] * bin_index[None, :] % pulse_count
    angles = product.astype(jnp.float32) * (2.0 * math.pi / pulse_count)
    cosine = jnp.cos(angles) / math.sqrt(pulse_count)
    sine = jnp.sin(angles) / math.sqrt(pulse_count)
    real_rows = jnp.concatenate([cosine, sine], axis=1)
    imag_rows = jnp.concatenate([-sine, cosine], axis=1)
    return jnp.stack([real_rows, imag_rows], axis=1).reshape(2 * pulse_count, 2 * pulse_count)


def doppler(turned):
    pulse_count = turned.shape[1]
    table = doppler_table(pulse_count)
    high_part = table.astype(jnp.bfloat16)
    low_part = (table - high_part.astype(jnp.float32)).astype(jnp.bfloat16)
    flat_data = turned.reshape(2 * pulse_count, -1)
    spectrum = jnp.dot(high_part, flat_data, preferred_element_type=jnp.float32)
    spectrum = spectrum + jnp.dot(low_part, flat_data, preferred_element_type=jnp.float32)
    return spectrum.astype(jnp.bfloat16).reshape(pulse_count, 2, turned.shape[2], turned.shape[3])


def add_terms(earlier, later):
    return earlier + later


def per_device(echoes, chirp, ridge, counts):
    tap_count = chirp.shape[1]
    pulse_local = echoes.shape[1]
    channel_count = echoes.shape[2]
    gate_local = echoes.shape[3]
    block_count = gate_local // tap_count
    previous = shifted(echoes[:, :, :, gate_local - tap_count :], "rng", 1)
    extended = jnp.concatenate([previous, echoes], axis=3)
    blocked = extended.reshape(2, pulse_local, channel_count, block_count + 1, tap_count)
    windows = jnp.concatenate([blocked[:, :, :, :-1], blocked[:, :, :, 1:]], axis=4)
    stacked = jnp.concatenate([windows[0], windows[1]], axis=3)
    table = filter_table(chirp, tap_count)
    filtered = jnp.dot(stacked, table, preferred_element_type=jnp.float32)
    compressed = jnp.stack([filtered[..., :tap_count], filtered[..., tap_count:]]).astype(
        jnp.bfloat16
    )
    compressed = compressed.reshape(2, pulse_local, channel_count, gate_local)
    spectra = lax.all_to_all(
        doppler(lax.all_to_all(compressed, "dop", split_axis=2, concat_axis=1, tiled=True)),
        "dop",
        split_axis=0,
        concat_axis=2,
        tiled=True,
    )
    bin_local = spectra.shape[0]
    snapshots = spectra.reshape(bin_local, 2 * channel_count, gate_local)
    block_index = jnp.arange(gate_local, dtype=jnp.int32) // TRAIN_BLK
    training = (block_index[None, :] < counts[:, None]).astype(jnp.bfloat16)
    masked = snapshots * training[:, None, :]
    rotated = jnp.concatenate([-masked[:, channel_count:], masked[:, :channel_count]], axis=1)
    paired = jnp.concatenate([masked, rotated], axis=2)
    gram = jnp.einsum("bkg,bjg->bkj", paired, paired, preferred_element_type=jnp.float32)
    segment = lax.axis_index("rng")
    before = prefix_2(gram, "rng", add_terms, jnp.zeros_like(gram))
    prefix = before + gram
    used = ((segment + 1) * counts * TRAIN_BLK).astype(jnp.float32)
    covariance = prefix / used[:, None, None]
    identity = jnp.eye(2 * channel_count, dtype=jnp.float32)
    loaded = (
        jnp.where(ridge[:, None, None] == 1, covariance, covariance * identity[None])
        + LOADING * identity[None]
    )
    factor = jnp.linalg.cholesky(loaded)
    solved = jax.scipy.linalg.solve_triangular(factor, snapshots.astype(jnp.float32), lower=True)
    return solved.astype(jnp.bfloat16)


def solution(mesh):
    in_specs = (P(None, "dop", None, "rng"), P(), P("dop"), P("dop"))
    out_specs = P("dop", None, "rng")
    return jax.shard_map(
        per_device, mesh=mesh, in_specs=in_specs, out_specs=out_specs, check_vma=False
    )
```

profile of v0, /device:TPU:0, one launch (start us, length us, event | category | flops | bytes accessed | tf_op | source)
XLA Modules:
  0.0 3021.7 jit_solution(1490069785957491038)
XLA Ops:
  47.0 26.0 pad_maximum_fusion
  73.1 69.2 %reshape.109 = bf16[2,32,64,9,512]{4,3,2,1,0:T(8,128)(2,1)} reshape(bf16[2,32,64,4608]{3,2,1,0:T(8,128)(2,1)} %pad_maximum_fusion) | data formatting | bytes 75497472 | tf_op jit(solution)/shard_map/reshape | solution.py:81
  142.3 52.8 %fusion.40 = (bf16[2,32,64,8,512]{4,3,2,1,0:T(8,128)(2,1)}, bf16[2,32,64,8,512]{4,3,2,1,0:T(8,128)(2,1)}) fusion(bf16[2,32,64,9,512]{4,3,2,1,0:T(8,128)(2,1)} %reshape.109), kind=kLoop, calls=%fused_computation.75 | loop fusion | bytes 134217728 | tf_op jit(solution)/shard_map/slice | solution.py:82
  195.2 44.2 %fusion.11 = (bf16[32,64,8,1024]{3,2,1,0:T(8,128)(2,1)}, bf16[32,64,8,1024]{3,2,1,0:T(8,128)(2,1)}) fusion(bf16[2,32,64,8,512]{4,3,2,1,0:T(8,128)(2,1)} %get-tuple-element.112, bf16[2,32,64,8,512]{4,3,2,1,0:T(8,128)(2,1)} %get-tuple-element.113), kind=kLoop, calls=%fused_computation.16 | loop fusion | flops 134217728 | bytes 134217728 | tf_op jit(solution)/shard_map/squeeze | solution.py:83
  239.4 76.4 %fusion.13 = bf16[32,64,8,1024]{3,2,1,0:T(8,128)(2,1)} fusion(bf16[32,64,8,1024]{3,2,1,0:T(8,128)(2,1)} %get-tuple-element.111, bf16[32,64,8,1024]{3,2,1,0:T(8,128)(2,1)} %get-tuple-element.110, bf16[1024,512]{1,0:T(8,128)(2,1)S(1)} %slice-done, bf16[1024,512]{1,0:T(8,128)(2,1)S(1)} %get-tuple-element.119, bf16[1024,512]{1,0:T(8,128)(2,1)S(1)} %get-tuple-element.118), kind=kOutput, calls=%fused_computation.21 | convolution fusion | flops 68887248896 | bytes 103809024 | tf_op jit(solution)/shard_map/dot_general | solution.py:85
  315.8 22.5 fusion.41
  338.2 25.5 stack.21
  382.2 25.5 stack.22
  426.5 23.0 pad_maximum_fusion.2
  461.9 706.4 %all-to-all-done = bf16[2,32,64,4096]{3,1,0,2:T(8,128)(2,1)} async-done(((bf16[2,32,64,4096]{3,1,0,2:T(8,128)(2,1)}), bf16[2,32,64,4096]{3,1,0,2:T(8,128)(2,1)}, u32[]{:S(2)}, u32[]{:S(2)}) %all-to-all-start) | async-done | bytes 33554464 | tf_op jit(solution)/shard_map/all_to_all | solution.py:91
  1168.3 29.4 copy.45
  1197.7 29.3 copy.56
  1227.0 40.6 %fusion.43 = f32[512,32768]{1,0:T(8,128)} fusion(bf16[512,512]{1,0:T(8,128)(2,1)S(1)} %convert_element_type.79, bf16[512,32768]{1,0:T(8,128)(2,1)} %bitcast.53), kind=kOutput, calls=%fused_computation.78 | convolution fusion | flops 17179869184 | bytes 101187584 | tf_op jit(solution)/shard_map/dot_general | solution.py:64
  1267.7 46.0 %add_convert_fusion = bf16[512,32768]{1,0:T(8,128)(2,1)} fusion(f32[512,32768]{1,0:T(8,128)} %fusion.43, bf16[512,512]{1,0:T(8,128)(2,1)S(1)} %convert_element_type.82, bf16[512,32768]{1,0:T(8,128)(2,1)} %bitcast.54), kind=kOutput, calls=%fused_computation.13 | convolution fusion | flops 17213423616 | bytes 134742016 | tf_op jit(solution)/shard_map/dot_general | solution.py:65
  1313.7 29.3 copy.57
  1359.4 720.7 %all-to-all-done.1 = bf16[256,2,8,4096]{3,2,1,0:T(8,128)(2,1)} async-done(((bf16[256,2,8,4096]{3,2,1,0:T(8,128)(2,1)}), bf16[256,2,8,4096]{3,2,1,0:T(8,128)(2,1)}, u32[]{:S(2)}, u32[]{:S(2)}) %all-to-all-start.1) | async-done | bytes 33554464 | tf_op jit(solution)/shard_map/all_to_all | solution.py:90
  2080.0 23.0 copy.46
  2103.1 23.3 broadcast_multiply_fusion
  2126.4 22.5 slice_negate_fusion
  2148.9 58.8 %fusion.4 = f32[32,128,128]{2,1,0:T(8,128)} fusion(bf16[32,64,4096]{2,1,0:T(8,128)(2,1)} %get-tuple-element.115, bf16[32,64,4096]{2,1,0:T(8,128)(2,1)} %get-tuple-element.114, bf16[32,128,4096]{2,1,0:T(8,128)(2,1)} %broadcast_multiply_fusion), kind=kOutput, calls=%fused_computation.7 | convolution fusion | flops 8791261184 | bytes 69206016 | tf_op jit(solution)/shard_map/bkg,bjg->bkj/dot_general | solution.py:104
  2211.0 58.0 %all-gather.3.cloned.1.call-done = f32[128,128,128]{2,1,0:T(8,128)} async-done(((f32[32,128,128]{2,1,0:T(8,128)}), f32[128,128,128]{2,1,0:T(8,128)}) %all-gather.3.cloned.1.call-update) | async-done | bytes 8388624 | tf_op jit(solution)/shard_map/all_gather | solution.py:22
  2287.9 375.8 %custom-call.8 = f32[32,128,128]{2,1,0:T(8,128)S(1)} custom-call(f32[32,128,128]{2,1,0:T(8,128)} %fusion.24), custom_call_target="Cholesky" | custom-call | tf_op jit(solution)/shard_map/jit(cholesky)/cholesky | solution.py:115
  2665.5 315.1 %custom-call.9 = f32[32,1,128,128]{2,3,1,0:T(8,128)S(1)} custom-call(f32[32,1,128,128]{3,2,1,0:T(8,128)} %select_bitcast_fusion), custom_call_target="InvertDiagBlocksLowerTriangular" | custom-call | tf_op jit(solution)/shard_map/jit(_solve_triangular)/vmap()/triangular_solve | solution.py:116
  2980.6 34.0 %convolution_convert_fusion = bf16[32,128,4096]{2,1,0:T(8,128)(2,1)} fusion(bf16[32,128,4096]{2,1,0:T(8,128)(2,1)} %bitcast.55, f32[32,1,128,128]{2,3,1,0:T(8,128)S(1)} %custom-call.9), kind=kOutput, calls=%fused_computation.20 | convolution fusion | flops 25786580992 | bytes 69206016 | tf_op jit(solution)/shard_map/jit(_solve_triangular)/vmap()/triangular_solve | solution.py:116
  (60 shorter events, 139.6 us)
Async XLA Ops:
  11.2 35.8 %collective-permute-start = (bf16[2,32,64,512]{3,2,1,0:T(8,128)(2,1)}, bf16[2,32,64,512]{3,2,1,0:T(8,128)(2,1)}, u32[]{:S(2)}, u32[]{:S(2)}) collective-permute-start(bf16[2,32,64,512]{3,2,1,0:T(8,128)(2,1)} %slice.59), channel_id=1, source_target_pairs={{0,1},{1,2},{2,3},{4,5},{5,6},{6,7},{8,9},{9,10},{10,11},{12,13},{... | collective-permute-start | bytes 12582920 | tf_op jit(solution)/shard_map/ppermute | solution.py:17
  195.1 44.2 %slice-start = ((bf16[1024,1535]{1,0:T(8,128)(2,1)}), bf16[1024,512]{1,0:T(8,128)(2,1)S(1)}, s32[]{:S(2)}) async-start(bf16[1024,1535]{1,0:T(8,128)(2,1)} %reshape.110), calls=%async_computation.3 | async-start | bytes 2097152 | tf_op jit(solution)/shard_map/slice | solution.py:39
  449.4 718.9 %all-to-all-start = ((bf16[2,32,64,4096]{3,1,0,2:T(8,128)(2,1)}), bf16[2,32,64,4096]{3,1,0,2:T(8,128)(2,1)}, u32[]{:S(2)}, u32[]{:S(2)}) async-start(bf16[2,32,64,4096]{3,1,0,2:T(8,128)(2,1)} %pad_maximum_fusion.2), calls=%async_computation | async-start | bytes 67108864 | tf_op jit(solution)/shard_map/all_to_all | solution.py:91
  1343.0 16.2 copy-start
  1343.0 737.0 %all-to-all-start.1 = ((bf16[256,2,8,4096]{3,2,1,0:T(8,128)(2,1)}), bf16[256,2,8,4096]{3,2,1,0:T(8,128)(2,1)}, u32[]{:S(2)}, u32[]{:S(2)}) async-start(bf16[256,2,8,4096]{3,2,1,0:T(8,128)(2,1)} %bitcast.57), calls=%async_computation.1 | async-start | bytes 67108864 | tf_op jit(solution)/shard_map/all_to_all | solution.py:90
  1359.2 909.8 %all-gather.3.cloned.1.call-start = ((), (), s32[]{:S(2)}) async-start(), calls=%async_computation.2 | async-start | bytes 10485760 | tf_op jit(solution)/shard_map/all_gather | solution.py:22
  2148.9 59.1 %copy-start.1 = (s32[32]{0:T(128)S(1)}, s32[32]{0:T(128)}, u32[]{:S(2)}) copy-start(s32[32]{0:T(128)} %param.8) | copy-start | bytes 388
Sparse Core Ops, SparseCore 0:
  2207.9 61.1 all-gather.2
where the time goes:
time: 3030 us; the launch traced here: 3020 us
  waiting for transfers between devices  1490 us (49%)
  other arithmetic  852 us (28%)
  local copies, waits for them, and re-layouts  387 us (13%)
  matrix products  256 us (8%)
    all_to_all x1, waiting for transfers between devices, per_device(): lax.all_to_all(doppler(lax.all_to_all(compressed, 'dop', split_axis=2, co...  721 us
    all_to_all x1, waiting for transfers between devices, per_device(): lax.all_to_all(compressed, 'dop', split_axis=2, concat_axis=1, tiled=True)  706 us
    another operation x4, other arithmetic, per_device(): factor = jnp.linalg.cholesky(loaded)  376 us
    another operation x3, other arithmetic, per_device(): jax.scipy.linalg.solve_triangular(factor, snapshots.astype(jnp.float32),...  317 us
    another operation x4, local copies, waits for them, and re-layouts, per_device(): jnp.stack([filtered[..., :tap_count], filtered[..., tap_count:]])  88.2 us
    dot_general x1, matrix products, per_device(): filtered = jnp.dot(stacked, table, preferred_element_type=jnp.float32)  76.4 us
    reshape x1, local copies, waits for them, and re-layouts, per_device(): extended.reshape(2, pulse_local, channel_count, block_count + 1, tap_count)  69.2 us
  transfers between devices with their start and end apart: 4, of which 3 were waited for; matrix products, arithmetic and copies ran while one was open for 1% of the time, Pallas kernels for 0%

commit v1 on v0

v1 whole, which is shorter than its diff:
```python
import functools
import math

import jax
import jax.numpy as jnp
import numpy as np
from jax import lax
from jax.experimental import pallas as pl
from jax.experimental.pallas import tpu as pltpu
from jax.sharding import PartitionSpec as P

TRAIN_BLK = 512
LOADING = 0.1
LANES = 128
WIDTH = 256
VMEM_LIMIT = 50 * 1024 * 1024

GATE_PLAN = (1, 6, 1)
BIN_PLAN = (4, 2, 1, 1)


def params():
    return pltpu.CompilerParams(vmem_limit_bytes=VMEM_LIMIT)


def cost(flops, nbytes):
    return pl.CostEstimate(flops=int(flops), bytes_accessed=int(nbytes), transcendentals=0)


def chunks(total, plan):
    unit = total // sum(plan)
    sizes = [unit * part for part in plan]
    starts = [sum(sizes[:k]) for k in range(len(sizes))]
    return list(zip(starts, sizes))


def table_kernel(taps, sequence_ref, table_ref):
    rows = taps + WIDTH
    length = sequence_ref.shape[1]
    tables = []
    for component in range(2):
        wide = jnp.broadcast_to(sequence_ref[component : component + 1, :], (rows, length))
        rolled = pltpu.roll(wide, 0, 1, stride=1, stride_axis=0)
        tables.append(rolled[:, :WIDTH])
    real, imag = tables
    table_ref[:rows, :WIDTH] = real.astype(table_ref.dtype)
    table_ref[:rows, WIDTH:] = imag.astype(table_ref.dtype)
    table_ref[rows:, :WIDTH] = (-imag).astype(table_ref.dtype)
    table_ref[rows:, WIDTH:] = real.astype(table_ref.dtype)


def filter_table(chirp):
    taps = chirp.shape[1]
    pad = taps + WIDTH - taps % WIDTH - WIDTH
    sequence = jnp.concatenate([jnp.zeros((2, pad), chirp.dtype), chirp], axis=1).astype(jnp.float32)
    return pl.pallas_call(
        functools.partial(table_kernel, taps),
        out_shape=jax.ShapeDtypeStruct((2 * (taps + WIDTH), 2 * WIDTH), chirp.dtype),
        compiler_params=params(),
        name="filter_table",
    )(sequence)


def compress_kernel(taps, has_halo, group, *refs):
    if has_halo:
        table_ref, halo_ref, before_ref, now_ref, out_ref, wide_ref = refs
    else:
        table_ref, before_ref, now_ref, out_ref, wide_ref = refs
    pulses, channels, gates = now_ref.shape[1:]
    rows = pulses * channels
    parts = []
    for component in range(2):
        before = before_ref[component]
        if has_halo:
            before = jnp.where(pl.program_id(1) == 0, halo_ref[component], before)
        parts.append(
            jnp.concatenate(
                [before.reshape(rows, taps), now_ref[component].reshape(rows, gates)], axis=1
            )
        )
    for tile in range(gates // WIDTH):
        first = tile * WIDTH
        window = jnp.concatenate([part[:, first : first + taps + WIDTH] for part in parts], axis=1)
        filtered = jnp.dot(window, table_ref[...], preferred_element_type=jnp.float32)
        per_part = WIDTH // LANES
        for lane_tile in range(2 * per_part):
            wide_ref[lane_tile] = filtered[:, lane_tile * LANES : (lane_tile + 1) * LANES]
        for channel in range(channels):
            for lane_tile in range(2 * per_part):
                component = lane_tile // per_part
                lanes = first + lane_tile % per_part * LANES
                piece = wide_ref[lane_tile, pl.ds(channel, pulses, stride=channels), :]
                out_ref[
                    channel // group,
                    channel % group,
                    component * pulses : (component + 1) * pulses,
                    lanes : lanes + LANES,
                ] = piece.astype(out_ref.dtype)


def compress(echoes, table, halo, start, size, groups):
    _, pulses, channels, gates = echoes.shape
    taps = table.shape[0] // 2 - WIDTH
    group = channels // groups
    at_once = max(16, group)
    step = taps
    offset = start // step
    has_halo = start == 0
    block = (2, pulses, at_once, step)
    in_specs = [pl.BlockSpec(table.shape, lambda c, g: (0, 0))]
    operands = [table]
    if has_halo:
        in_specs.append(pl.BlockSpec(block, lambda c, g: (0, 0, c, 0)))
        operands.append(halo)
    in_specs.append(pl.BlockSpec(block, lambda c, g: (0, 0, c, jnp.maximum(offset + g - 1, 0))))
    in_specs.append(pl.BlockSpec(block, lambda c, g: (0, 0, c, offset + g)))
    operands += [echoes, echoes]
    return pl.pallas_call(
        functools.partial(compress_kernel, taps, has_halo, group),
        grid=(channels // at_once, size // step),
        in_specs=in_specs,
        out_specs=pl.BlockSpec(
            (at_once // group, group, 2 * pulses, step), lambda c, g: (c, 0, 0, g)
        ),
        out_shape=jax.ShapeDtypeStruct((groups, group, 2 * pulses, size), echoes.dtype),
        scratch_shapes=[pltpu.VMEM((2 * WIDTH // LANES, pulses * at_once, LANES), jnp.float32)],
        compiler_params=params(),
        cost_estimate=cost(
            2 * pulses * channels * size * (taps + WIDTH) * 4, 12 * pulses * channels * size
        ),
        name="compress",
    )(*operands)


def doppler_tables(pulse_count, groups):
    index = np.arange(pulse_count, dtype=np.int64)
    angles = (index[:, None] * index[None, :] % pulse_count) * (2.0 * math.pi / pulse_count)
    cosine = np.cos(angles) / math.sqrt(pulse_count)
    sine = np.sin(angles) / math.sqrt(pulse_count)
    local = pulse_count // groups
    cosine = cosine.reshape(pulse_count, groups, 1, local)
    sine = sine.reshape(pulse_count, groups, 1, local)
    real_rows = np.concatenate([cosine, sine], axis=2).reshape(pulse_count, 2 * pulse_count)
    imag_rows = np.concatenate([-sine, cosine], axis=2).reshape(pulse_count, 2 * pulse_count)
    table = np.concatenate([real_rows, imag_rows], axis=0)
    high = table.astype(jnp.bfloat16)
    low = (table - high.astype(np.float64)).astype(jnp.bfloat16)
    return jnp.asarray(high), jnp.asarray(low)


def doppler_kernel(plan, carried, *refs):
    high_ref, low_ref, in_ref = refs[:3]
    outs = refs[3 + carried : 3 + carried + len(plan)]
    wide_ref = refs[-1]
    groups, group, depth, gates = in_ref.shape
    total = groups * depth
    bins = total // 2
    local = bins // groups
    for channel in range(group):
        data = in_ref[:, channel].reshape(total, gates)
        spectrum = jnp.dot(high_ref[...], data, preferred_element_type=jnp.float32)
        spectrum = spectrum + jnp.dot(low_ref[...], data, preferred_element_type=jnp.float32)
        for lane_tile in range(gates // LANES):
            wide_ref[lane_tile, channel * total : (channel + 1) * total, :] = spectrum[
                :, lane_tile * LANES : (lane_tile + 1) * LANES
            ]
    for out_ref, (first, count) in zip(outs, plan):
        for place in range(groups):

            def move(k, carry, out_ref=out_ref, base=place * local + first, place=place):
                for lane_tile in range(gates // LANES):
                    real = wide_ref[lane_tile, pl.ds(base + k, group, stride=total), :]
                    imag = wide_ref[lane_tile, pl.ds(base + k + bins, group, stride=total), :]
                    out_ref[place, k, :, lane_tile * LANES : (lane_tile + 1) * LANES] = (
                        jnp.concatenate([real, imag], axis=0).astype(out_ref.dtype)
                    )
                return carry

            lax.fori_loop(0, count, move, 0, unroll=True)


def doppler(received, tables, earlier, start, gates, plan):
    groups, group, depth, size = received.shape
    total = groups * depth
    step = WIDTH
    offset = start // step
    table_spec = pl.BlockSpec((total, total), lambda g: (0, 0))
    in_specs = [
        table_spec,
        table_spec,
        pl.BlockSpec((groups, group, depth, step), lambda g: (0, 0, 0, g)),
    ]
    operands = [*tables, received]
    aliases = {}
    if earlier is not None:
        for k, array in enumerate(earlier):
            aliases[len(operands)] = k
            operands.append(array)
            in_specs.append(pl.BlockSpec(memory_space=pl.ANY))
    return pl.pallas_call(
        functools.partial(doppler_kernel, plan, 0 if earlier is None else len(earlier)),
        grid=(size // step,),
        in_specs=in_specs,
        out_specs=[
            pl.BlockSpec((groups, count, 2 * group, step), lambda g: (0, 0, 0, offset + g))
            for _, count in plan
        ],
        out_shape=[
            jax.ShapeDtypeStruct((groups, count, 2 * group, gates), received.dtype)
            for _, count in plan
        ],
        scratch_shapes=[pltpu.VMEM((step // LANES, group * total, LANES), jnp.float32)],
        input_output_aliases=aliases,
        compiler_params=params(),
        cost_estimate=cost(4 * total * total * group * size, 4 * total * group * size),
        name="doppler",
    )(*operands)


def doppler_plain(received, tables, plan):
    groups, group, depth, size = received.shape
    total = groups * depth
    data = jnp.moveaxis(received, 1, 2).reshape(total, group * size)
    spectrum = jnp.dot(tables[0], data, preferred_element_type=jnp.float32)
    spectrum = spectrum + jnp.dot(tables[1], data, preferred_element_type=jnp.float32)
    spectrum = spectrum.astype(received.dtype).reshape(2, groups, depth // 2, group, size)
    spectrum = spectrum.transpose(1, 2, 0, 3, 4).reshape(groups, depth // 2, 2 * group, size)
    return [spectrum[:, first : first + count] for first, count in plan]


def natural_rows(matrix, groups):
    half = matrix.shape[0] // groups // 2
    pieces = [matrix[2 * half * s : 2 * half * s + half] for s in range(groups)]
    pieces += [matrix[2 * half * s + half : 2 * half * (s + 1)] for s in range(groups)]
    return jnp.concatenate(pieces, axis=0)


def grouped_rows(matrix, groups):
    rows = matrix.shape[0]
    half = rows // groups // 2
    pieces = []
    for s in range(groups):
        pieces.append(matrix[half * s : half * (s + 1)])
        pieces.append(matrix[rows // 2 + half * s : rows // 2 + half * (s + 1)])
    return jnp.concatenate(pieces, axis=0)


def gram_kernel(counts_ref, data_ref, out_ref, total_ref):
    groups, _, rows, gates = data_ref.shape
    size = groups * rows
    total_ref[...] = jnp.zeros_like(total_ref)
    count = counts_ref[pl.program_id(0)]
    for block in range(gates // TRAIN_BLK):

        @pl.when(block < count)
        def _():
            data = data_ref[:, 0, :, block * TRAIN_BLK : (block + 1) * TRAIN_BLK]
            data = data.reshape(size, TRAIN_BLK)
            total_ref[...] += lax.dot_general(
                data, data, (((1,), (1,)), ((), ())), preferred_element_type=jnp.float32
            )

    gram = natural_rows(natural_rows(total_ref[...], groups).T, groups)
    half = size // 2
    lane = lax.broadcasted_iota(jnp.int32, (half, size), 1)
    turned = pltpu.roll(gram[half:], half, 1)
    out_ref[0] = gram[:half] + jnp.where(lane < half, turned, -turned)


def gram(data, counts):
    groups, bins, rows, gates = data.shape
    size = groups * rows
    return pl.pallas_call(
        gram_kernel,
        grid_spec=pltpu.PrefetchScalarGridSpec(
            num_scalar_prefetch=1,
            grid=(bins,),
            in_specs=[pl.BlockSpec((groups, 1, rows, gates), lambda b, counts: (0, b, 0, 0))],
            out_specs=pl.BlockSpec((1, size // 2, size), lambda b, counts: (b, 0, 0)),
            scratch_shapes=[pltpu.VMEM((size, size), jnp.float32)],
        ),
        out_shape=jax.ShapeDtypeStruct((bins, size // 2, size), jnp.float32),
        compiler_params=params(),
        cost_estimate=cost(2 * bins * size * size * gates, 2 * bins * size * gates),
        name="gram",
    )(counts, data)


def factor_kernel(groups, segment_ref, counts_ref, ridge_ref, grams_ref, out_ref, work_ref, inverse_ref):
    segments, bins, half, size = grams_ref.shape
    segment = segment_ref[0]
    lane = lax.broadcasted_iota(jnp.int32, (half, size), 1)
    row = lax.broadcasted_iota(jnp.int32, (size, size), 0)
    column = lax.broadcasted_iota(jnp.int32, (size, size), 1)
    for b in range(bins):
        top = grams_ref[0, b]
        for t in range(1, segments):
            top = jnp.where(t <= segment, top + grams_ref[t, b], top)
        turned = pltpu.roll(top, half, 1)
        full = jnp.concatenate([top, jnp.where(lane < half, -turned, turned)], axis=0)
        used = ((segment + 1) * counts_ref[b] * TRAIN_BLK).astype(jnp.float32)
        covariance = full / used
        kept = jnp.logical_or(ridge_ref[b] == 1, row == column)
        work_ref[b] = jnp.where(kept, covariance, 0.0) + jnp.where(row == column, LOADING, 0.0)

    one_lane = lax.broadcasted_iota(jnp.int32, (1, size), 1)
    parts = 4
    for part in range(parts):
        low = part * size // parts
        lanes = lax.broadcasted_iota(jnp.int32, (size - low, size), 1)

        def step(j, carry, low=low, lanes=lanes):
            here = one_lane == j
            mask = lanes == j
            rows = [work_ref[b, pl.ds(j, 1), :] for b in range(bins)]
            pivots = [jnp.sum(jnp.where(here, row, 0.0), axis=1, keepdims=True) for row in rows]
            for b in range(bins):
                kept = jnp.where(one_lane < j, rows[b], jnp.where(here, 1.0, 0.0))
                inverse_ref[b, pl.ds(j, 1), :] = kept * lax.rsqrt(pivots[b])
            scaled = [jnp.where(here, 1.0, row) / pivot for row, pivot in zip(rows, pivots)]
            for b in range(bins):
                matrix = work_ref[b, low:, :]
                entries = jnp.sum(jnp.where(mask, matrix, 0.0), axis=1, keepdims=True)
                work_ref[b, low:, :] = jnp.where(mask, 0.0, matrix) - entries * scaled[b]
            return carry

        lax.fori_loop(low, low + size // parts, step, 0)
    for b in range(bins):
        inverse = grouped_rows(inverse_ref[b].T, groups).T
        high = inverse.astype(jnp.bfloat16)
        out_ref[b, :, :size] = high
        out_ref[b, :, size:] = (inverse - high.astype(jnp.float32)).astype(jnp.bfloat16)


def inverse_factors(grams, segment, counts, ridge, groups):
    segments, bins, half, size = grams.shape
    smem = pl.BlockSpec(memory_space=pltpu.SMEM)
    return pl.pallas_call(
        functools.partial(factor_kernel, groups),
        in_specs=[smem, smem, smem, pl.BlockSpec(memory_space=pltpu.VMEM)],
        out_specs=pl.BlockSpec(memory_space=pltpu.VMEM),
        out_shape=jax.ShapeDtypeStruct((bins, size, 2 * size), jnp.bfloat16),
        scratch_shapes=[
            pltpu.VMEM((bins, size, size), jnp.float32),
            pltpu.VMEM((bins, size, size), jnp.float32),
        ],
        compiler_params=params(),
        cost_estimate=cost(2 * bins * size**3 * 20, 4 * segments * bins * half * size),
        name="inverse_factors",
    )(segment, counts, ridge, grams)


def whiten_kernel(inverse_ref, data_ref, *refs):
    out_ref = refs[-1]
    groups, _, rows, gates = data_ref.shape
    size = groups * rows
    step = 1024 if gates % 1024 == 0 else gates
    for first in range(0, gates, step):
        data = data_ref[:, 0, :, first : first + step].reshape(size, step)
        twice = jnp.concatenate([data, data], axis=0)
        out_ref[0, :, first : first + step] = jnp.dot(
            inverse_ref[0], twice, preferred_element_type=jnp.float32
        ).astype(out_ref.dtype)


def whiten(inverse, data, earlier, first, total):
    groups, bins, rows, gates = data.shape
    size = groups * rows
    in_specs = [
        pl.BlockSpec((1, size, 2 * size), lambda b: (b, 0, 0)),
        pl.BlockSpec((groups, 1, rows, gates), lambda b: (0, b, 0, 0)),
    ]
    operands = [inverse, data]
    aliases = {}
    if earlier is not None:
        in_specs.append(pl.BlockSpec(memory_space=pl.ANY))
        operands.append(earlier)
        aliases = {2: 0}
    return pl.pallas_call(
        whiten_kernel,
        grid=(bins,),
        in_specs=in_specs,
        out_specs=pl.BlockSpec((1, size, gates), lambda b: (first + b, 0, 0)),
        out_shape=jax.ShapeDtypeStruct((total, size, gates), data.dtype),
        input_output_aliases=aliases,
        compiler_params=params(),
        cost_estimate=cost(4 * bins * size * size * gates, 4 * bins * size * gates),
        name="whiten",
    )(*operands)


def exchange(array):
    return lax.all_to_all(array, "dop", split_axis=0, concat_axis=0, tiled=True)


def per_device(echoes, chirp, ridge, counts):
    taps = chirp.shape[1]
    _, pulses, channels, gates = echoes.shape
    groups = lax.axis_size("dop")
    group = channels // groups
    pulse_count = pulses * groups
    bins = counts.shape[0]
    bin_plan = chunks(bins, BIN_PLAN)
    gate_plan = [(gates - start - size, size) for start, size in chunks(gates, GATE_PLAN)]

    segments = lax.axis_size("rng")
    route = [(k, k + 1) for k in range(segments - 1)]
    halo = lax.ppermute(echoes[:, :, :, gates - taps :], "rng", route)
    table = filter_table(chirp)
    tables = doppler_tables(pulse_count, groups)

    received = []
    for start, size in gate_plan:
        received.append(exchange(compress(echoes, table, halo, start, size, groups)))

    if group % 8 == 0:
        spectra = None
        for (start, size), part in zip(gate_plan, received):
            spectra = doppler(part, tables, spectra, start, gates, bin_plan)
    else:
        pieces = [doppler_plain(part, tables, bin_plan) for part in received]
        spectra = [jnp.concatenate(piece[::-1], axis=3) for piece in zip(*pieces)]

    segment = lax.axis_index("rng").reshape(1)
    whitened = None
    data = exchange(spectra[0])
    for k, (first, count) in enumerate(bin_plan):
        if k + 1 < len(bin_plan):
            if whitened is None:
                following, data = lax.optimization_barrier((spectra[k + 1], data))
            else:
                following, data, whitened = lax.optimization_barrier(
                    (spectra[k + 1], data, whitened)
                )
            following = exchange(following)
        if group % 8:
            data = data.reshape(groups, count, 2, group, gates).transpose(1, 2, 0, 3, 4)
            data = data.reshape(1, count, 2 * channels, gates)
        these = counts[first : first + count]
        grams = lax.all_gather(gram(data, these), "rng")
        inverse = inverse_factors(
            grams, segment, these, ridge[first : first + count], data.shape[0]
        )
        whitened = whiten(inverse, data, whitened, first, bins)
        data = following
    return whitened


def solution(mesh):
    in_specs = (P(None, "dop", None, "rng"), P(), P("dop"), P("dop"))
    out_specs = P("dop", None, "rng")
    return jax.shard_map(
        per_device, mesh=mesh, in_specs=in_specs, out_specs=out_specs, check_vma=False
    )
```

time: 3030 us -> 1570 us (0.52)
  other arithmetic: 852 us -> 0.69 us
  waiting for transfers between devices: 1490 us -> 777 us
  blocking collectives: 0 us -> 383 us
  local copies, waits for them, and re-layouts: 387 us -> 7.79 us
  Pallas kernels: 0 us -> 354 us
  matrix products: 256 us -> 0 us
    another operation x9 -> x0, other arithmetic: 716 us -> none  [the longest x4 376 us: per_device(): factor = jnp.linalg.cholesky(loaded)]
    all_to_all x2 -> x6, waiting for transfers between devices: 1430 us -> 725 us  [exchange(): return lax.all_to_all(array, 'dop', split_axis=0, concat_axis=0, tiled=True)]
    all_to_all x0 -> x1, blocking collectives: none -> 369 us  [exchange(): return lax.all_to_all(array, 'dop', split_axis=0, concat_axis=0, tiled=True)]
    pallas_call x0 -> x19, Pallas kernels: none -> 354 us  [the longest x4 93.8 us: inverse_factors(): pl.pallas_call(functools.partial(factor_kernel, groups), in_specs=[smem,...]
    dot_general x4 -> x0, matrix products: 222 us -> none  [the longest x1 76.4 us: per_device(): filtered = jnp.dot(stacked, table, preferred_element_type=jnp.float32)]
    another operation x10 -> x0, local copies, waits for them, and re-layouts: 100 us -> none  [the longest x4 88.2 us: per_device(): jnp.stack([filtered[..., :tap_count], filtered[..., tap_count:]])]
    reshape x3 -> x0, local copies, waits for them, and re-layouts: 83 us -> none  [the longest x1 69.2 us: per_device(): extended.reshape(2, pulse_local, channel_count, block_count + 1, tap_count)]
    slice x8 -> x5, local copies, waits for them, and re-layouts: 85.5 us -> 2.96 us  [the longest x1 2.68 us: per_device(): halo = lax.ppermute(echoes[:, :, :, gates - taps:], 'rng', route)]
  transfers between devices with their start and end apart: 4 -> 9, of which waited for: 3 -> 9; matrix products, arithmetic and copies ran while one was open for 1% -> 0% of each run, Pallas kernels for 0% -> 19%
where the time goes in v1:
time: 1570 us
  waiting for transfers between devices  777 us (49%)
  blocking collectives  383 us (24%)
  Pallas kernels  354 us (23%)
  starting transfers between devices  34.3 us (2%)
    all_to_all x6, waiting for transfers between devices, exchange(): return lax.all_to_all(array, 'dop', split_axis=0, concat_axis=0, tiled=True)  725 us
    all_to_all x1, blocking collectives, exchange(): return lax.all_to_all(array, 'dop', split_axis=0, concat_axis=0, tiled=True)  369 us
    pallas_call x4, Pallas kernels, inverse_factors(): pl.pallas_call(functools.partial(factor_kernel, groups), in_specs=[smem,...  93.8 us
    pallas_call x3, Pallas kernels, doppler(): pl.pallas_call(functools.partial(doppler_kernel, plan, 0 if earlier is No...  86.4 us
    pallas_call x3, Pallas kernels, compress(): pl.pallas_call(functools.partial(compress_kernel, taps, has_halo, group),...  86.1 us
    pallas_call x4, Pallas kernels, gram(): pl.pallas_call(gram_kernel, grid_spec=pltpu.PrefetchScalarGridSpec(num_sc...  45 us
    all_gather x2, waiting for transfers between devices, per_device(): grams = lax.all_gather(gram(data, these), 'rng')  44.7 us
    pallas_call x4, Pallas kernels, whiten(): pl.pallas_call(whiten_kernel, grid=(bins,), in_specs=in_specs, out_specs=...  41.9 us
  transfers between devices with their start and end apart: 9, of which 9 were waited for; matrix products, arithmetic and copies ran while one was open for 0% of the time, Pallas kernels for 19%

profile of v1, /device:TPU:0, one launch (start us, length us, event | category | flops | bytes accessed | tf_op | source)
XLA Modules:
  0.0 1569.8 jit_solution(17535496882275317077)
XLA Ops:
  7.5 12.2 compress.5
  19.7 7.3 all-to-all-start.2
  27.0 61.3 %compress.4 = bf16[8,8,64,3072]{3,2,1,0:T(8,128)(2,1)} custom-call(bf16[1536,512]{1,0:T(8,128)(2,1)S(1)} %filter_table.1.refs_0_, bf16[2,32,64,4096]{3,2,1,0:T(8,128)(2,1)} %refs_2_.5, bf16[2,32,64,4096]{3,2,1,0:T(8,128)(2,1)} %refs_2_.5), custom_call_target="tpu_custom_call" | custom-call | flops 38654705664 | bytes 75497472 | tf_op jit(solution)/shard_map/compress/pallas_call | solution.py:118
  88.3 32.0 %all-to-all-done.2.refs_2_ = bf16[8,8,64,512]{3,2,1,0:T(8,128)(2,1)} async-done(((bf16[8,8,64,512]{3,2,1,0:T(8,128)(2,1)}), bf16[8,8,64,512]{3,2,1,0:T(8,128)(2,1)}, u32[]{:S(2)}, u32[]{:S(2)}) %all-to-all-start.2) | async-done | bytes 4194336 | tf_op jit(solution)/shard_map/all_to_all | solution.py:393
  139.4 12.6 compress.3
  152.0 516.3 %all-to-all-done.1.refs_2_ = bf16[8,8,64,3072]{3,2,1,0:T(8,128)(2,1)} async-done(((bf16[8,8,64,3072]{3,2,1,0:T(8,128)(2,1)}), bf16[8,8,64,3072]{3,2,1,0:T(8,128)(2,1)}, u32[]{:S(2)}, u32[]{:S(2)}) %all-to-all-start.1) | async-done | bytes 25165856 | tf_op jit(solution)/shard_map/all_to_all | solution.py:393
  673.1 12.6 doppler.3
  685.8 61.3 %doppler.4 = (bf16[8,16,16,4096]{3,2,1,0:T(8,128)(2,1)}, bf16[8,8,16,4096]{3,2,1,0:T(8,128)(2,1)}, bf16[8,4,16,4096]{3,2,1,0:T(8,128)(2,1)}, bf16[8,4,16,4096]{3,2,1,0:T(8,128)(2,1)}) custom-call(bf16[512,512]{1,0:T(8,128)(2,1)S(1)} %copy-done, ...), custom_call_target="tpu_custom_call", output_to_operand_aliasing={{0}: (3, {}), {1}: (4, {}), {2}: (5, {}), {3}: (6, {})} | custom-call | flops 25769803776 | bytes 50331648 | tf_op jit(solution)/shard_map/doppler/pallas_call | solution.py:200
  747.0 18.6 %all-to-all-done.refs_2_ = bf16[8,8,64,512]{3,2,1,0:T(8,128)(2,1)} async-done(((bf16[8,8,64,512]{3,2,1,0:T(8,128)(2,1)}), bf16[8,8,64,512]{3,2,1,0:T(8,128)(2,1)}, u32[]{:S(2)}, u32[]{:S(2)}) %all-to-all-start) | async-done | bytes 4194336 | tf_op jit(solution)/shard_map/all_to_all | solution.py:393
  765.6 12.6 doppler.5
  778.2 368.8 %all_to_all.35.data_ref = bf16[8,16,16,4096]{3,2,1,0:T(8,128)(2,1)} all-to-all(bf16[8,16,16,4096]{3,2,1,0:T(8,128)(2,1)} %get-tuple-element.36), channel_id=1, replica_groups=mesh['dop'=8,'rng'=4] {'dop'}, dimensions={0} | all-to-all | bytes 33554432 | tf_op jit(solution)/shard_map/all_to_all | solution.py:393
  1152.2 22.1 %gram.4 = f32[16,64,128]{2,1,0:T(8,128)} custom-call(s32[16]{0:T(128)S(1)} %bitcast.9, bf16[8,16,16,4096]{3,2,1,0:T(8,128)(2,1)} %all_to_all.35.data_ref), custom_call_target="tpu_custom_call" | custom-call | flops 2147483648 | bytes 16777216 | tf_op jit(solution)/shard_map/gram/pallas_call | solution.py:273
  1174.3 24.3 %all-gather.7.cloned.1.call-done = f32[64,64,128]{2,1,0:T(8,128)} async-done(((f32[16,64,128]{2,1,0:T(8,128)}), f32[64,64,128]{2,1,0:T(8,128)}) %all-gather.7.cloned.1.call-update) | async-done | bytes 2097168 | tf_op jit(solution)/shard_map/all_gather | solution.py:440
  1200.2 35.6 %inverse_factors.4.inverse_ref = bf16[16,128,256]{2,1,0:T(8,128)(2,1)S(1)} custom-call(s32[1]{0:T(128)} %bitcast.segment_ref, s32[16]{0:T(128)S(1)} %bitcast.10, s32[16]{0:T(128)S(1)} %bitcast.11, f32[4,16,64,128]{3,2,1,0:T(8,128)S(1)} %bitcast.12), custom_call_target="tpu_custom_call" | custom-call | flops 1342177280 | bytes 2097152 | tf_op jit(solution)/shard_map/inverse_factors/pallas_call | solution.py:338
  1235.8 20.3 %whiten.4.refs_0_ = bf16[32,128,4096]{2,1,0:T(8,128)(2,1)} custom-call(bf16[16,128,256]{2,1,0:T(8,128)(2,1)S(1)} %inverse_factors.4.inverse_ref, bf16[8,16,16,4096]{3,2,1,0:T(8,128)(2,1)} %all_to_all.35.data_ref), custom_call_target="tpu_custom_call" | custom-call | flops 4294967296 | bytes 33554432 | tf_op jit(solution)/shard_map/whiten/pallas_call | solution.py:379
  1256.1 77.4 %all-to-all-done.4.data_ref = bf16[8,8,16,4096]{3,2,1,0:T(8,128)(2,1)} async-done(((bf16[8,8,16,4096]{3,2,1,0:T(8,128)(2,1)}), bf16[8,8,16,4096]{3,2,1,0:T(8,128)(2,1)}, u32[]{:S(2)}, u32[]{:S(2)}) %all-to-all-start.4) | async-done | bytes 8388640 | tf_op jit(solution)/shard_map/all_to_all | solution.py:393
  1338.2 11.7 gram.5
  1350.0 20.4 %all-gather.9.cloned.1.call-done = f32[32,64,128]{2,1,0:T(8,128)} async-done(((f32[8,64,128]{2,1,0:T(8,128)}), f32[32,64,128]{2,1,0:T(8,128)}) %all-gather.9.cloned.1.call-update) | async-done | bytes 1048592 | tf_op jit(solution)/shard_map/all_gather | solution.py:440
  1371.7 23.4 %inverse_factors.5.inverse_ref = bf16[8,128,256]{2,1,0:T(8,128)(2,1)S(1)} custom-call(s32[1]{0:T(128)} %bitcast.segment_ref, s32[8]{0:T(128)S(1)} %slice.32.counts_ref, s32[8]{0:T(128)S(1)} %slice.33.ridge_ref, f32[4,8,64,128]{3,2,1,0:T(8,128)S(1)} %bitcast.13), custom_call_target="tpu_custom_call" | custom-call | flops 671088640 | bytes 1048576 | tf_op jit(solution)/shard_map/inverse_factors/pallas_call | solution.py:338
  1395.1 10.5 whiten.5.refs_0_
  1405.6 24.9 %all-to-all-done.5.data_ref = bf16[8,4,16,4096]{3,2,1,0:T(8,128)(2,1)} async-done(((bf16[8,4,16,4096]{3,2,1,0:T(8,128)(2,1)}), bf16[8,4,16,4096]{3,2,1,0:T(8,128)(2,1)}, u32[]{:S(2)}, u32[]{:S(2)}) %all-to-all-start.5) | async-done | bytes 4194336 | tf_op jit(solution)/shard_map/all_to_all | solution.py:393
  1448.2 17.5 %inverse_factors.7.inverse_ref = bf16[4,128,256]{2,1,0:T(8,128)(2,1)S(1)} custom-call(s32[1]{0:T(128)} %bitcast.segment_ref, s32[4]{0:T(128)S(1)} %get-tuple-element.47.counts_ref, s32[4]{0:T(128)S(1)} %get-tuple-element.45.ridge_ref, f32[4,4,64,128]{3,2,1,0:T(8,128)S(1)} %bitcast.8), custom_call_target="tpu_custom_call" | custom-call | flops 335544320 | bytes 524288 | tf_op jit(solution)/shard_map/inverse_factors/pallas_call | solution.py:338
  1471.4 56.2 %all-to-all-done.6.data_ref = bf16[8,4,16,4096]{3,2,1,0:T(8,128)(2,1)} async-done(((bf16[8,4,16,4096]{3,2,1,0:T(8,128)(2,1)}), bf16[8,4,16,4096]{3,2,1,0:T(8,128)(2,1)}, u32[]{:S(2)}, u32[]{:S(2)}) %all-to-all-start.6) | async-done | bytes 4194336 | tf_op jit(solution)/shard_map/all_to_all | solution.py:393
  1540.2 17.3 %inverse_factors.6.inverse_ref = bf16[4,128,256]{2,1,0:T(8,128)(2,1)S(1)} custom-call(s32[1]{0:T(128)} %bitcast.segment_ref, s32[4]{0:T(128)S(1)} %get-tuple-element.48.counts_ref, s32[4]{0:T(128)S(1)} %get-tuple-element.46.ridge_ref, f32[4,4,64,128]{3,2,1,0:T(8,128)S(1)} %bitcast.7), custom_call_target="tpu_custom_call" | custom-call | flops 335544320 | bytes 524288 | tf_op jit(solution)/shard_map/inverse_factors/pallas_call | solution.py:338
  (38 shorter events, 79.1 us)
Async XLA Ops:
  19.7 100.5 %all-to-all-start.2 = ((bf16[8,8,64,512]{3,2,1,0:T(8,128)(2,1)}), bf16[8,8,64,512]{3,2,1,0:T(8,128)(2,1)}, u32[]{:S(2)}, u32[]{:S(2)}) async-start(bf16[8,8,64,512]{3,2,1,0:T(8,128)(2,1)} %compress.5), calls=%async_computation.2 | async-start | bytes 8388608 | tf_op jit(solution)/shard_map/all_to_all | solution.py:393
  120.2 548.1 %all-to-all-start.1 = ((bf16[8,8,64,3072]{3,2,1,0:T(8,128)(2,1)}), bf16[8,8,64,3072]{3,2,1,0:T(8,128)(2,1)}, u32[]{:S(2)}, u32[]{:S(2)}) async-start(bf16[8,8,64,3072]{3,2,1,0:T(8,128)(2,1)} %compress.4), calls=%async_computation.1 | async-start | bytes 50331648 | tf_op jit(solution)/shard_map/all_to_all | solution.py:393
  129.3 8.1 collective-permute-start
  137.4 2.0 copy-start.6
  152.0 521.1 %copy-start = (bf16[512,512]{1,0:T(8,128)(2,1)S(1)}, bf16[512,512]{1,0:T(8,128)(2,1)}, u32[]{:S(2)}) copy-start(bf16[512,512]{1,0:T(8,128)(2,1)} %constant.10.clone.refs_0_) | copy-start | bytes 1572868
  152.0 521.1 %copy-start.1 = (bf16[512,512]{1,0:T(8,128)(2,1)S(1)}, bf16[512,512]{1,0:T(8,128)(2,1)}, u32[]{:S(2)}) copy-start(bf16[512,512]{1,0:T(8,128)(2,1)} %constant.11.clone.refs_1_) | copy-start | bytes 1572868
  668.4 97.2 %all-to-all-start = ((bf16[8,8,64,512]{3,2,1,0:T(8,128)(2,1)}), bf16[8,8,64,512]{3,2,1,0:T(8,128)(2,1)}, u32[]{:S(2)}, u32[]{:S(2)}) async-start(bf16[8,8,64,512]{3,2,1,0:T(8,128)(2,1)} %compress.3), calls=%async_computation | async-start | bytes 8388608 | tf_op jit(solution)/shard_map/all_to_all | solution.py:393
  1147.0 5.2 copy-start.2
  1147.0 186.5 %all-to-all-start.4 = ((bf16[8,8,16,4096]{3,2,1,0:T(8,128)(2,1)}), bf16[8,8,16,4096]{3,2,1,0:T(8,128)(2,1)}, u32[]{:S(2)}, u32[]{:S(2)}) async-start(bf16[8,8,16,4096]{3,2,1,0:T(8,128)(2,1)} %get-tuple-element.37), calls=%async_computation.4 | async-start | bytes 16777216 | tf_op jit(solution)/shard_map/all_to_all | solution.py:393
  1152.1 46.5 %all-gather.7.cloned.1.call-start = ((), (), s32[]{:S(2)}) async-start(), calls=%async_computation.7 | async-start | bytes 2621440 | tf_op jit(solution)/shard_map/all_gather | solution.py:440
  1152.2 46.5 %copy-start.3 = (s32[32]{0:T(128)S(1)}, s32[32]{0:T(128)}, u32[]{:S(2)}) copy-start(s32[32]{0:T(128)} %param.8) | copy-start | bytes 388
  1198.6 1.6 copy-start.4
  1333.5 97.0 %all-to-all-start.5 = ((bf16[8,4,16,4096]{3,2,1,0:T(8,128)(2,1)}), bf16[8,4,16,4096]{3,2,1,0:T(8,128)(2,1)}, u32[]{:S(2)}, u32[]{:S(2)}) async-start(bf16[8,4,16,4096]{3,2,1,0:T(8,128)(2,1)} %get-tuple-element.39), calls=%async_computation.5 | async-start | bytes 8388608 | tf_op jit(solution)/shard_map/all_to_all | solution.py:393
  1338.1 32.4 %all-gather.9.cloned.1.call-start = ((), (), s32[]{:S(2)}) async-start(), calls=%async_computation.8 | async-start | bytes 1310720 | tf_op jit(solution)/shard_map/all_gather | solution.py:440
  1370.4 1.2 copy-start.5
  1430.5 97.1 %all-to-all-start.6 = ((bf16[8,4,16,4096]{3,2,1,0:T(8,128)(2,1)}), bf16[8,4,16,4096]{3,2,1,0:T(8,128)(2,1)}, u32[]{:S(2)}, u32[]{:S(2)}) async-start(bf16[8,4,16,4096]{3,2,1,0:T(8,128)(2,1)} %get-tuple-element.42), calls=%async_computation.6 | async-start | bytes 8388608 | tf_op jit(solution)/shard_map/all_to_all | solution.py:393
Sparse Core Ops, SparseCore 0:
  1174.5 24.1 all-gather.6
  1350.0 20.3 all-gather.8

commit v2 on v1

--- a/solution.py
+++ b/solution.py
@@ -16,7 +16,7 @@
 VMEM_LIMIT = 50 * 1024 * 1024
 
 GATE_PLAN = (1, 6, 1)
-BIN_PLAN = (4, 2, 1, 1)
+BIN_PLAN = (12, 3, 1)
 
 
 def params():
@@ -28,8 +28,8 @@
 
 
 def chunks(total, plan):
-    unit = total // sum(plan)
-    sizes = [unit * part for part in plan]
+    sizes = [max(1, total * part // sum(plan)) for part in plan]
+    sizes[0] = total - sum(sizes[1:])
     starts = [sum(sizes[:k]) for k in range(len(sizes))]
     return list(zip(starts, sizes))
 
@@ -161,7 +161,7 @@
         spectrum = jnp.dot(high_ref[...], data, preferred_element_type=jnp.float32)
         spectrum = spectrum + jnp.dot(low_ref[...], data, preferred_element_type=jnp.float32)
         for lane_tile in range(gates // LANES):
-            wide_ref[lane_tile, channel * total : (channel + 1) * total, :] = spectrum[
+            wide_ref[lane_tile, pl.ds(channel, total, stride=group), :] = spectrum[
                 :, lane_tile * LANES : (lane_tile + 1) * LANES
             ]
     for out_ref, (first, count) in zip(outs, plan):
@@ -169,8 +169,8 @@
 
             def move(k, carry, out_ref=out_ref, base=place * local + first, place=place):
                 for lane_tile in range(gates // LANES):
-                    real = wide_ref[lane_tile, pl.ds(base + k, group, stride=total), :]
-                    imag = wide_ref[lane_tile, pl.ds(base + k + bins, group, stride=total), :]
+                    real = wide_ref[lane_tile, pl.ds((base + k) * group, group), :]
+                    imag = wide_ref[lane_tile, pl.ds((base + k + bins) * group, group), :]
                     out_ref[place, k, :, lane_tile * LANES : (lane_tile + 1) * LANES] = (
                         jnp.concatenate([real, imag], axis=0).astype(out_ref.dtype)
                     )
@@ -401,7 +401,10 @@
     pulse_count = pulses * groups
     bins = counts.shape[0]
     bin_plan = chunks(bins, BIN_PLAN)
-    gate_plan = [(gates - start - size, size) for start, size in chunks(gates, GATE_PLAN)]
+    gate_plan = [
+        (gates - taps * (start + size), taps * size)
+        for start, size in chunks(gates // taps, GATE_PLAN)
+    ]
 
     segments = lax.axis_size("rng")
     route = [(k, k + 1) for k in range(segments - 1)]

time: 1570 us -> 1560 us (level)
  blocking collectives: 383 us -> 565 us
  waiting for transfers between devices: 777 us -> 633 us
  Pallas kernels: 354 us -> 309 us
    all_to_all x1, blocking collectives: 369 us -> 550 us  [exchange(): return lax.all_to_all(array, 'dop', split_axis=0, concat_axis=0, tiled=True)]
    all_to_all x6 -> x5, waiting for transfers between devices: 725 us -> 599 us  [exchange(): return lax.all_to_all(array, 'dop', split_axis=0, concat_axis=0, tiled=True)]
    pallas_call x3, Pallas kernels: 86.4 us -> 52.7 us  [doppler(): pl.pallas_call(functools.partial(doppler_kernel, plan, 0 if earlier is No...]
    all_gather x2 -> x1, waiting for transfers between devices: 44.7 us -> 28 us  [per_device(): grams = lax.all_gather(gram(data, these), 'rng')]
    pallas_call x4 -> x3, Pallas kernels: 93.8 us -> 83.9 us  [inverse_factors(): pl.pallas_call(functools.partial(factor_kernel, groups), in_specs=[smem,...]
    all_to_all x6 -> x5, starting transfers between devices: 32.7 us -> 28.9 us  [exchange(): return lax.all_to_all(array, 'dop', split_axis=0, concat_axis=0, tiled=True)]
    pallas_call x4 -> x3, Pallas kernels: 41.9 us -> 40.2 us  [whiten(): pl.pallas_call(whiten_kernel, grid=(bins,), in_specs=in_specs, out_specs=...]
    pallas_call x4 -> x3, Pallas kernels: 45 us -> 45.6 us  [gram(): pl.pallas_call(gram_kernel, grid_spec=pltpu.PrefetchScalarGridSpec(num_sc...]
  transfers between devices with their start and end apart: 9 -> 7, of which waited for: 9 -> 6; matrix products, arithmetic and copies ran while one was open for 0% -> 0% of each run, Pallas kernels for 19% -> 17%
where the time goes in v2:
time: 1560 us
  waiting for transfers between devices  633 us (41%)
  blocking collectives  565 us (36%)
  Pallas kernels  309 us (20%)
  starting transfers between devices  30.5 us (2%)
    all_to_all x5, waiting for transfers between devices, exchange(): return lax.all_to_all(array, 'dop', split_axis=0, concat_axis=0, tiled=True)  599 us
    all_to_all x1, blocking collectives, exchange(): return lax.all_to_all(array, 'dop', split_axis=0, concat_axis=0, tiled=True)  550 us
    pallas_call x3, Pallas kernels, compress(): pl.pallas_call(functools.partial(compress_kernel, taps, has_halo, group),...  86.1 us
    pallas_call x3, Pallas kernels, inverse_factors(): pl.pallas_call(functools.partial(factor_kernel, groups), in_specs=[smem,...  83.9 us
    pallas_call x3, Pallas kernels, doppler(): pl.pallas_call(functools.partial(doppler_kernel, plan, 0 if earlier is No...  52.7 us
    pallas_call x3, Pallas kernels, gram(): pl.pallas_call(gram_kernel, grid_spec=pltpu.PrefetchScalarGridSpec(num_sc...  45.6 us
    pallas_call x3, Pallas kernels, whiten(): pl.pallas_call(whiten_kernel, grid=(bins,), in_specs=in_specs, out_specs=...  40.2 us
  transfers between devices with their start and end apart: 7, of which 6 were waited for; matrix products, arithmetic and copies ran while one was open for 0% of the time, Pallas kernels for 17%

profile of v2, /device:TPU:0, one launch (start us, length us, event | category | flops | bytes accessed | tf_op | source)
XLA Modules:
  0.0 1556.6 jit_solution(15975187752917361488)
XLA Ops:
  7.5 12.2 compress.5
  19.7 7.3 all-to-all-start.2
  27.0 61.3 %compress.4 = bf16[8,8,64,3072]{3,2,1,0:T(8,128)(2,1)} custom-call(bf16[1536,512]{1,0:T(8,128)(2,1)S(1)} %filter_table.1.refs_0_, bf16[2,32,64,4096]{3,2,1,0:T(8,128)(2,1)} %refs_2_.5, bf16[2,32,64,4096]{3,2,1,0:T(8,128)(2,1)} %refs_2_.5), custom_call_target="tpu_custom_call" | custom-call | flops 38654705664 | bytes 75497472 | tf_op jit(solution)/shard_map/compress/pallas_call | solution.py:118
  88.3 32.0 %all-to-all-done.2.refs_2_ = bf16[8,8,64,512]{3,2,1,0:T(8,128)(2,1)} async-done(((bf16[8,8,64,512]{3,2,1,0:T(8,128)(2,1)}), bf16[8,8,64,512]{3,2,1,0:T(8,128)(2,1)}, u32[]{:S(2)}, u32[]{:S(2)}) %all-to-all-start.2) | async-done | bytes 4194336 | tf_op jit(solution)/shard_map/all_to_all | solution.py:393
  120.3 6.5 all-to-all-start.1
  131.0 6.5 collective-permute-done.refs_1_
  139.4 12.6 compress.3
  152.0 516.5 %all-to-all-done.1.refs_2_ = bf16[8,8,64,3072]{3,2,1,0:T(8,128)(2,1)} async-done(((bf16[8,8,64,3072]{3,2,1,0:T(8,128)(2,1)}), bf16[8,8,64,3072]{3,2,1,0:T(8,128)(2,1)}, u32[]{:S(2)}, u32[]{:S(2)}) %all-to-all-start.1) | async-done | bytes 25165856 | tf_op jit(solution)/shard_map/all_to_all | solution.py:393
  673.2 8.4 doppler.3
  681.6 35.9 %doppler.4 = (bf16[8,24,16,4096]{3,2,1,0:T(8,128)(2,1)}, bf16[8,6,16,4096]{3,2,1,0:T(8,128)(2,1)}, bf16[8,2,16,4096]{3,2,1,0:T(8,128)(2,1)S(1)}) custom-call(bf16[512,512]{1,0:T(8,128)(2,1)S(1)} %copy-done.1, bf16[512,512]{1,0:T(8,128)(2,1)S(1)} %copy-done.2, ...), custom_call_target="tpu_custom_call", output_to_operand_aliasing={{0}: (3, {}), {1}: (4, {}), {2}: (5, {})} | custom-call | flops 25769803776 | bytes 50331648 | tf_op jit(solution)/shard_map/doppler/pallas_call | solution.py:200
  717.6 48.1 %all-to-all-done.refs_2_ = bf16[8,8,64,512]{3,2,1,0:T(8,128)(2,1)} async-done(((bf16[8,8,64,512]{3,2,1,0:T(8,128)(2,1)}), bf16[8,8,64,512]{3,2,1,0:T(8,128)(2,1)}, u32[]{:S(2)}, u32[]{:S(2)}) %all-to-all-start) | async-done | bytes 4194336 | tf_op jit(solution)/shard_map/all_to_all | solution.py:393
  765.6 8.4 doppler.5
  774.0 550.4 %all_to_all.30.data_ref = bf16[8,24,16,4096]{3,2,1,0:T(8,128)(2,1)} all-to-all(bf16[8,24,16,4096]{3,2,1,0:T(8,128)(2,1)} %get-tuple-element.27), channel_id=1, replica_groups=mesh['dop'=8,'rng'=4] {'dop'}, dimensions={0} | all-to-all | bytes 50331648 | tf_op jit(solution)/shard_map/all_to_all | solution.py:393
  1329.4 34.3 %gram.3 = f32[24,64,128]{2,1,0:T(8,128)} custom-call(s32[24]{0:T(128)S(1)} %bitcast.8, bf16[8,24,16,4096]{3,2,1,0:T(8,128)(2,1)} %all_to_all.30.data_ref), custom_call_target="tpu_custom_call" | custom-call | flops 3221225472 | bytes 25165824 | tf_op jit(solution)/shard_map/gram/pallas_call | solution.py:273
  1363.7 28.0 %all-gather.5.cloned.1.call-done = f32[96,64,128]{2,1,0:T(8,128)} async-done(((f32[24,64,128]{2,1,0:T(8,128)}), f32[96,64,128]{2,1,0:T(8,128)}) %all-gather.5.cloned.1.call-update) | async-done | bytes 3145744 | tf_op jit(solution)/shard_map/all_gather | solution.py:443
  1391.7 49.1 %inverse_factors.3.inverse_ref = bf16[24,128,256]{2,1,0:T(8,128)(2,1)S(1)} custom-call(s32[1]{0:T(128)} %bitcast.segment_ref, s32[24]{0:T(128)S(1)} %bitcast.9, s32[24]{0:T(128)S(1)} %bitcast.10, f32[4,24,64,128]{3,2,1,0:T(8,128)} %bitcast.11), custom_call_target="tpu_custom_call" | custom-call | flops 2013265920 | bytes 3145728 | tf_op jit(solution)/shard_map/inverse_factors/pallas_call | solution.py:338
  1440.9 30.0 %whiten.3.refs_0_ = bf16[32,128,4096]{2,1,0:T(8,128)(2,1)} custom-call(bf16[24,128,256]{2,1,0:T(8,128)(2,1)S(1)} %inverse_factors.3.inverse_ref, bf16[8,24,16,4096]{3,2,1,0:T(8,128)(2,1)} %all_to_all.30.data_ref), custom_call_target="tpu_custom_call" | custom-call | flops 6442450944 | bytes 50331648 | tf_op jit(solution)/shard_map/whiten/pallas_call | solution.py:379
  1470.9 5.5 all-to-all-start.5
  1476.7 8.9 gram.5
  1485.6 8.6 all-gather.2
  1494.2 20.4 %inverse_factors.5.inverse_ref = bf16[6,128,256]{2,1,0:T(8,128)(2,1)S(1)} custom-call(s32[1]{0:T(128)} %bitcast.segment_ref, s32[6]{0:T(128)S(1)} %slice.26.counts_ref, s32[6]{0:T(128)S(1)} %slice.27.ridge_ref, f32[4,6,64,128]{3,2,1,0:T(8,128)S(1)} %bitcast.6), custom_call_target="tpu_custom_call" | custom-call | flops 503316480 | bytes 786432 | tf_op jit(solution)/shard_map/inverse_factors/pallas_call | solution.py:338
  1514.6 8.1 whiten.4.refs_0_
  1527.5 5.8 all-gather.1
  1533.3 14.3 inverse_factors.4.inverse_ref
  (28 shorter events, 24.1 us)
Async XLA Ops:
  19.7 100.5 %all-to-all-start.2 = ((bf16[8,8,64,512]{3,2,1,0:T(8,128)(2,1)}), bf16[8,8,64,512]{3,2,1,0:T(8,128)(2,1)}, u32[]{:S(2)}, u32[]{:S(2)}) async-start(bf16[8,8,64,512]{3,2,1,0:T(8,128)(2,1)} %compress.5), calls=%async_computation.2 | async-start | bytes 8388608 | tf_op jit(solution)/shard_map/all_to_all | solution.py:393
  120.3 548.2 %all-to-all-start.1 = ((bf16[8,8,64,3072]{3,2,1,0:T(8,128)(2,1)}), bf16[8,8,64,3072]{3,2,1,0:T(8,128)(2,1)}, u32[]{:S(2)}, u32[]{:S(2)}) async-start(bf16[8,8,64,3072]{3,2,1,0:T(8,128)(2,1)} %compress.4), calls=%async_computation.1 | async-start | bytes 50331648 | tf_op jit(solution)/shard_map/all_to_all | solution.py:393
  129.4 8.1 collective-permute-start
  137.5 1.9 copy-start.5
  152.0 521.2 %copy-start.1 = (bf16[512,512]{1,0:T(8,128)(2,1)S(1)}, bf16[512,512]{1,0:T(8,128)(2,1)}, u32[]{:S(2)}) copy-start(bf16[512,512]{1,0:T(8,128)(2,1)} %constant.10.clone.refs_0_) | copy-start | bytes 1572868
  152.0 521.2 %copy-start.2 = (bf16[512,512]{1,0:T(8,128)(2,1)S(1)}, bf16[512,512]{1,0:T(8,128)(2,1)}, u32[]{:S(2)}) copy-start(bf16[512,512]{1,0:T(8,128)(2,1)} %constant.11.clone.refs_1_) | copy-start | bytes 1572868
  668.5 97.1 %all-to-all-start = ((bf16[8,8,64,512]{3,2,1,0:T(8,128)(2,1)}), bf16[8,8,64,512]{3,2,1,0:T(8,128)(2,1)}, u32[]{:S(2)}, u32[]{:S(2)}) async-start(bf16[8,8,64,512]{3,2,1,0:T(8,128)(2,1)} %compress.3), calls=%async_computation | async-start | bytes 8388608 | tf_op jit(solution)/shard_map/all_to_all | solution.py:393
  774.0 550.4 %copy-start = (bf16[8,2,16,4096]{3,2,1,0:T(8,128)(2,1)}, bf16[8,2,16,4096]{3,2,1,0:T(8,128)(2,1)S(1)}, u32[]{:S(2)}) copy-start(bf16[8,2,16,4096]{3,2,1,0:T(8,128)(2,1)S(1)} %get-tuple-element.30) | copy-start | bytes 6291460
  1324.4 5.0 copy-start.3
  1324.4 146.5 %all-to-all-start.4 = ((bf16[8,6,16,4096]{3,2,1,0:T(8,128)(2,1)}), bf16[8,6,16,4096]{3,2,1,0:T(8,128)(2,1)}, u32[]{:S(2)}, u32[]{:S(2)}) async-start(bf16[8,6,16,4096]{3,2,1,0:T(8,128)(2,1)} %get-tuple-element.28), calls=%async_computation.4 | async-start | bytes 12582912 | tf_op jit(solution)/shard_map/all_to_all | solution.py:393
  1329.3 62.4 %all-gather.5.cloned.1.call-start = ((), (), s32[]{:S(2)}) async-start(), calls=%async_computation.6 | async-start | bytes 3932160 | tf_op jit(solution)/shard_map/all_gather | solution.py:443
  1329.4 62.3 %copy-start.4 = (s32[32]{0:T(128)S(1)}, s32[32]{0:T(128)}, u32[]{:S(2)}) copy-start(s32[32]{0:T(128)} %param.8) | copy-start | bytes 388
  1470.9 54.2 %all-to-all-start.5 = ((bf16[8,2,16,4096]{3,2,1,0:T(8,128)(2,1)}), bf16[8,2,16,4096]{3,2,1,0:T(8,128)(2,1)S(1)}, u32[]{:S(2)}, u32[]{:S(2)}) async-start(bf16[8,2,16,4096]{3,2,1,0:T(8,128)(2,1)} %copy-done), calls=%async_computation.5 | async-start | bytes 4194304 | tf_op jit(solution)/shard_map/all_to_all | solution.py:393
Sparse Core Ops, SparseCore 0:
  1363.8 27.8 all-gather.4

commit v3 on v2

--- a/solution.py
+++ b/solution.py
@@ -12,6 +12,8 @@
 TRAIN_BLK = 512
 LOADING = 0.1
 LANES = 128
+BINS_AT_ONCE = 4
+PANEL = 16
 WIDTH = 256
 VMEM_LIMIT = 50 * 1024 * 1024
 
@@ -245,41 +247,48 @@
     return jnp.concatenate(pieces, axis=0)
 
 
-def gram_kernel(counts_ref, data_ref, out_ref, total_ref):
-    groups, _, rows, gates = data_ref.shape
+def gram_kernel(counts_ref, data_ref, out_ref):
+    groups, bins, rows, gates = data_ref.shape
     size = groups * rows
-    total_ref[...] = jnp.zeros_like(total_ref)
-    count = counts_ref[pl.program_id(0)]
-    for block in range(gates // TRAIN_BLK):
-
-        @pl.when(block < count)
-        def _():
-            data = data_ref[:, 0, :, block * TRAIN_BLK : (block + 1) * TRAIN_BLK]
-            data = data.reshape(size, TRAIN_BLK)
-            total_ref[...] += lax.dot_general(
-                data, data, (((1,), (1,)), ((), ())), preferred_element_type=jnp.float32
-            )
-
-    gram = natural_rows(natural_rows(total_ref[...], groups).T, groups)
-    half = size // 2
+    half, quarter = size // 2, size // 4
+    row = lax.broadcasted_iota(jnp.int32, (half, size), 0)
     lane = lax.broadcasted_iota(jnp.int32, (half, size), 1)
-    turned = pltpu.roll(gram[half:], half, 1)
-    out_ref[0] = gram[:half] + jnp.where(lane < half, turned, -turned)
+    gate = lax.broadcasted_iota(jnp.int32, (size, gates), 1)
+    for b in range(bins):
+        training = counts_ref[pl.program_id(0) * bins + b] * TRAIN_BLK
+        data = data_ref[:, b].reshape(size, gates)
+        data = jnp.where(gate < training, data, jnp.zeros_like(data))
+        gram = lax.dot_general(
+            data, data, (((1,), (1,)), ((), ())), preferred_element_type=jnp.float32
+        )
+        gram = natural_rows(natural_rows(gram, groups).T, groups)
+        turned = pltpu.roll(gram[half:], half, 1)
+        top = gram[:half] + jnp.where(lane < half, turned, -turned)
+        packed = jnp.where(row >= lane, top, pltpu.roll(top, half, 1))
+        out_ref[b] = jnp.where(
+            lane[:quarter] < half, packed[:quarter], pltpu.roll(packed[quarter:], half, 1)
+        )
+
+
+def per_step(bins):
+    return next(k for k in (BINS_AT_ONCE, 2, 1) if bins % k == 0)
 
 
 def gram(data, counts):
     groups, bins, rows, gates = data.shape
     size = groups * rows
+    at_once = per_step(bins)
     return pl.pallas_call(
         gram_kernel,
         grid_spec=pltpu.PrefetchScalarGridSpec(
             num_scalar_prefetch=1,
-            grid=(bins,),
-            in_specs=[pl.BlockSpec((groups, 1, rows, gates), lambda b, counts: (0, b, 0, 0))],
-            out_specs=pl.BlockSpec((1, size // 2, size), lambda b, counts: (b, 0, 0)),
-            scratch_shapes=[pltpu.VMEM((size, size), jnp.float32)],
+            grid=(bins // at_once,),
+            in_specs=[
+                pl.BlockSpec((groups, at_once, rows, gates), lambda b, counts: (0, b, 0, 0))
+            ],
+            out_specs=pl.BlockSpec((at_once, size // 4, size), lambda b, counts: (b, 0, 0)),
         ),
-        out_shape=jax.ShapeDtypeStruct((bins, size // 2, size), jnp.float32),
+        out_shape=jax.ShapeDtypeStruct((bins, size // 4, size), jnp.float32),
         compiler_params=params(),
         cost_estimate=cost(2 * bins * size * size * gates, 2 * bins * size * gates),
         name="gram",
@@ -287,88 +296,142 @@
 
 
 def factor_kernel(groups, segment_ref, counts_ref, ridge_ref, grams_ref, out_ref, work_ref, inverse_ref):
-    segments, bins, half, size = grams_ref.shape
+    segments, bins, quarter, size = grams_ref.shape
+    half = size // 2
     segment = segment_ref[0]
     lane = lax.broadcasted_iota(jnp.int32, (half, size), 1)
     row = lax.broadcasted_iota(jnp.int32, (size, size), 0)
     column = lax.broadcasted_iota(jnp.int32, (size, size), 1)
+    inner_row = jnp.where(row < half, row, row - half)
+    inner_column = jnp.where(column < half, column, column - half)
+    lower = inner_row >= inner_column
+    diagonal = inner_row == inner_column
+    upper_side = jnp.logical_and(row < half, column >= half)
+    lower_side = jnp.logical_and(row >= half, column < half)
+    side = jnp.logical_or(upper_side, lower_side)
     for b in range(bins):
-        top = grams_ref[0, b]
+        total = grams_ref[0, b]
         for t in range(1, segments):
-            top = jnp.where(t <= segment, top + grams_ref[t, b], top)
-        turned = pltpu.roll(top, half, 1)
-        full = jnp.concatenate([top, jnp.where(lane < half, -turned, turned)], axis=0)
+            total = jnp.where(t <= segment, total + grams_ref[t, b], total)
+        packed = jnp.concatenate([total, pltpu.roll(total, half, 1)], axis=0)
+        packed = jnp.where(lane < half, packed, pltpu.roll(packed, half, 1))
+        packed = jnp.concatenate([packed, packed], axis=0)
+        turned = packed.T
+        symmetric = jnp.where(lower, packed, turned)
+        skew = jnp.where(diagonal, 0.0, jnp.where(lower, -turned, packed))
+        full = jnp.where(side, jnp.where(lower_side, -skew, skew), symmetric)
         used = ((segment + 1) * counts_ref[b] * TRAIN_BLK).astype(jnp.float32)
         covariance = full / used
         kept = jnp.logical_or(ridge_ref[b] == 1, row == column)
         work_ref[b] = jnp.where(kept, covariance, 0.0) + jnp.where(row == column, LOADING, 0.0)
 
     one_lane = lax.broadcasted_iota(jnp.int32, (1, size), 1)
-    parts = 4
-    for part in range(parts):
-        low = part * size // parts
-        lanes = lax.broadcasted_iota(jnp.int32, (size - low, size), 1)
-
-        def step(j, carry, low=low, lanes=lanes):
-            here = one_lane == j
-            mask = lanes == j
-            rows = [work_ref[b, pl.ds(j, 1), :] for b in range(bins)]
-            pivots = [jnp.sum(jnp.where(here, row, 0.0), axis=1, keepdims=True) for row in rows]
+    panel = min(PANEL if bins > 8 else 2 * PANEL, size)
+    panel_lane = lax.broadcasted_iota(jnp.int32, (panel, size), 1)
+    panel_row = lax.broadcasted_iota(jnp.int32, (panel, size), 0)
+    for low in range(0, size, panel):
+        high = low + panel
+
+        def step(k, carry, low=low, high=high):
+            j = low + 2 * k
+            first_lane, second_lane = one_lane == j, one_lane == j + 1
+            first_mask, second_mask = panel_lane == j, panel_lane == j + 1
+            scales, units = [], []
             for b in range(bins):
-                kept = jnp.where(one_lane < j, rows[b], jnp.where(here, 1.0, 0.0))
-                inverse_ref[b, pl.ds(j, 1), :] = kept * lax.rsqrt(pivots[b])
-            scaled = [jnp.where(here, 1.0, row) / pivot for row, pivot in zip(rows, pivots)]
+                row = work_ref[b, pl.ds(j, 1), :]
+                following = work_ref[b, pl.ds(j + 1, 1), :]
+                pivot = jnp.sum(jnp.where(first_lane, row, 0.0), axis=1, keepdims=True)
+                link = jnp.sum(jnp.where(second_lane, row, 0.0), axis=1, keepdims=True)
+                corner = jnp.sum(jnp.where(second_lane, following, 0.0), axis=1, keepdims=True)
+                root = lax.rsqrt(pivot)
+                ratio = link * (root * root)
+                second_root = lax.rsqrt(corner - ratio * link)
+                unit = jnp.where(first_lane, 1.0, row)
+                second = jnp.where(first_lane, 0.0, following) - ratio * unit
+                second = jnp.where(second_lane, 1.0, second)
+                scales.append((root, ratio, second_root))
+                units.append((unit, second))
             for b in range(bins):
-                matrix = work_ref[b, low:, :]
-                entries = jnp.sum(jnp.where(mask, matrix, 0.0), axis=1, keepdims=True)
-                work_ref[b, low:, :] = jnp.where(mask, 0.0, matrix) - entries * scaled[b]
+                root, ratio, second_root = scales[b]
+                unit, second = units[b]
+                inverse_ref[b, pl.ds(j, 1), :] = unit * root
+                inverse_ref[b, pl.ds(j + 1, 1), :] = second * second_root
+            for b in range(bins):
+                root, ratio, second_root = scales[b]
+                unit, second = units[b]
+                matrix = work_ref[b, low:high, :]
+                entries = jnp.sum(jnp.where(first_mask, matrix, 0.0), axis=1, keepdims=True)
+                others = jnp.sum(jnp.where(second_mask, matrix, 0.0), axis=1, keepdims=True)
+                others = (others - entries * ratio) * (second_root * second_root)
+                entries = entries * (root * root)
+                matrix = jnp.where(jnp.logical_or(first_mask, second_mask), 0.0, matrix)
+                work_ref[b, low:high, :] = (
+                    matrix - entries * jnp.where(second_lane, 0.0, unit) - others * second
+                )
             return carry
 
-        lax.fori_loop(low, low + size // parts, step, 0)
+        lax.fori_loop(0, panel // 2, step, 0)
+        if high < size:
+            inside = jnp.logical_and(panel_lane > panel_row + low, panel_lane < high)
+            below_lane = lax.broadcasted_iota(jnp.int32, (size - high, size), 1)
+            cleared = jnp.logical_and(below_lane >= low, below_lane < high)
+            for b in range(bins):
+                rows = inverse_ref[b, low:high, :]
+                product = jnp.dot(
+                    rows.T[high:],
+                    jnp.where(inside, 0.0, rows),
+                    preferred_element_type=jnp.float32,
+                    precision=lax.Precision.HIGHEST,
+                )
+                work_ref[b, high:, :] = (
+                    jnp.where(cleared, 0.0, work_ref[b, high:, :]) - product
+                )
+    for b in range(bins):
+        inverse_ref[b] = jnp.where(column <= row, inverse_ref[b], 0.0)
     for b in range(bins):
         inverse = grouped_rows(inverse_ref[b].T, groups).T
         high = inverse.astype(jnp.bfloat16)
-        out_ref[b, :, :size] = high
-        out_ref[b, :, size:] = (inverse - high.astype(jnp.float32)).astype(jnp.bfloat16)
+        out_ref[b, :size, :] = high
+        out_ref[b, size:, :] = (inverse - high.astype(jnp.float32)).astype(jnp.bfloat16)
 
 
 def inverse_factors(grams, segment, counts, ridge, groups):
-    segments, bins, half, size = grams.shape
+    segments, bins, quarter, size = grams.shape
     smem = pl.BlockSpec(memory_space=pltpu.SMEM)
     return pl.pallas_call(
         functools.partial(factor_kernel, groups),
         in_specs=[smem, smem, smem, pl.BlockSpec(memory_space=pltpu.VMEM)],
         out_specs=pl.BlockSpec(memory_space=pltpu.VMEM),
-        out_shape=jax.ShapeDtypeStruct((bins, size, 2 * size), jnp.bfloat16),
+        out_shape=jax.ShapeDtypeStruct((bins, 2 * size, size), jnp.bfloat16),
         scratch_shapes=[
             pltpu.VMEM((bins, size, size), jnp.float32),
             pltpu.VMEM((bins, size, size), jnp.float32),
         ],
         compiler_params=params(),
-        cost_estimate=cost(2 * bins * size**3 * 20, 4 * segments * bins * half * size),
+        cost_estimate=cost(2 * bins * size**3 * 20, 4 * segments * bins * quarter * size),
         name="inverse_factors",
     )(segment, counts, ridge, grams)
 
 
 def whiten_kernel(inverse_ref, data_ref, *refs):
     out_ref = refs[-1]
-    groups, _, rows, gates = data_ref.shape
+    groups, bins, rows, gates = data_ref.shape
     size = groups * rows
     step = 1024 if gates % 1024 == 0 else gates
-    for first in range(0, gates, step):
-        data = data_ref[:, 0, :, first : first + step].reshape(size, step)
-        twice = jnp.concatenate([data, data], axis=0)
-        out_ref[0, :, first : first + step] = jnp.dot(
-            inverse_ref[0], twice, preferred_element_type=jnp.float32
-        ).astype(out_ref.dtype)
+    for b in range(bins):
+        for first in range(0, gates, step):
+            data = data_ref[:, b, :, first : first + step].reshape(size, step)
+            both = jnp.dot(inverse_ref[b], data, preferred_element_type=jnp.float32)
+            out_ref[b, :, first : first + step] = (both[:size] + both[size:]).astype(out_ref.dtype)
 
 
 def whiten(inverse, data, earlier, first, total):
     groups, bins, rows, gates = data.shape
     size = groups * rows
+    at_once = next(k for k in (BINS_AT_ONCE, 2, 1) if bins % k == 0 and first % k == 0)
     in_specs = [
-        pl.BlockSpec((1, size, 2 * size), lambda b: (b, 0, 0)),
-        pl.BlockSpec((groups, 1, rows, gates), lambda b: (0, b, 0, 0)),
+        pl.BlockSpec((at_once, 2 * size, size), lambda b: (b, 0, 0)),
+        pl.BlockSpec((groups, at_once, rows, gates), lambda b: (0, b, 0, 0)),
     ]
     operands = [inverse, data]
     aliases = {}
@@ -378,9 +441,9 @@
         aliases = {2: 0}
     return pl.pallas_call(
         whiten_kernel,
-        grid=(bins,),
+        grid=(bins // at_once,),
         in_specs=in_specs,
-        out_specs=pl.BlockSpec((1, size, gates), lambda b: (first + b, 0, 0)),
+        out_specs=pl.BlockSpec((at_once, size, gates), lambda b: (first // at_once + b, 0, 0)),
         out_shape=jax.ShapeDtypeStruct((total, size, gates), data.dtype),
         input_output_aliases=aliases,
         compiler_params=params(),

time: 1560 us -> 1540 us (0.987)
  Pallas kernels: 309 us -> 242 us
  waiting for transfers between devices: 633 us -> 689 us
    all_to_all x5, waiting for transfers between devices: 599 us -> 662 us  [exchange(): return lax.all_to_all(array, 'dop', split_axis=0, concat_axis=0, tiled=True)]
    pallas_call x3, Pallas kernels: 83.9 us -> 47.3 us  [inverse_factors(): pl.pallas_call(functools.partial(factor_kernel, groups), in_specs=[smem,...]
    pallas_call x3, Pallas kernels: 45.6 us -> 21.8 us  [gram(): pl.pallas_call(gram_kernel, grid_spec=pltpu.PrefetchScalarGridSpec(num_sc...]
  transfers between devices with their start and end apart: 7 -> 7, of which waited for: 6 -> 7; matrix products, arithmetic and copies ran while one was open for 0% -> 0% of each run, Pallas kernels for 17% -> 13%
where the time goes in v3:
time: 1540 us
  waiting for transfers between devices  689 us (45%)
  blocking collectives  562 us (36%)
  Pallas kernels  242 us (16%)
  starting transfers between devices  29.1 us (2%)
    all_to_all x5, waiting for transfers between devices, exchange(): return lax.all_to_all(array, 'dop', split_axis=0, concat_axis=0, tiled=True)  662 us
    all_to_all x1, blocking collectives, exchange(): return lax.all_to_all(array, 'dop', split_axis=0, concat_axis=0, tiled=True)  550 us
    pallas_call x3, Pallas kernels, compress(): pl.pallas_call(functools.partial(compress_kernel, taps, has_halo, group),...  86.1 us
    pallas_call x3, Pallas kernels, doppler(): pl.pallas_call(functools.partial(doppler_kernel, plan, 0 if earlier is No...  52.7 us
    pallas_call x3, Pallas kernels, inverse_factors(): pl.pallas_call(functools.partial(factor_kernel, groups), in_specs=[smem,...  47.3 us
    pallas_call x3, Pallas kernels, whiten(): pl.pallas_call(whiten_kernel, grid=(bins // at_once,), in_specs=in_specs,...  33.8 us
  transfers between devices with their start and end apart: 7, of which 7 were waited for; matrix products, arithmetic and copies ran while one was open for 0% of the time, Pallas kernels for 13%

profile of v3, /device:TPU:0, one launch (start us, length us, event | category | flops | bytes accessed | tf_op | source)
XLA Modules:
  0.0 1543.1 jit_solution(9494825520523863054)
XLA Ops:
  7.5 12.2 compress.5
  19.7 7.3 all-to-all-start.2
  27.0 61.3 %compress.4 = bf16[8,8,64,3072]{3,2,1,0:T(8,128)(2,1)} custom-call(bf16[1536,512]{1,0:T(8,128)(2,1)S(1)} %filter_table.1.refs_0_, bf16[2,32,64,4096]{3,2,1,0:T(8,128)(2,1)} %refs_2_.5, bf16[2,32,64,4096]{3,2,1,0:T(8,128)(2,1)} %refs_2_.5), custom_call_target="tpu_custom_call" | custom-call | flops 38654705664 | bytes 75497472 | tf_op jit(solution)/shard_map/compress/pallas_call | solution.py:120
  88.3 32.0 %all-to-all-done.2.refs_2_ = bf16[8,8,64,512]{3,2,1,0:T(8,128)(2,1)} async-done(((bf16[8,8,64,512]{3,2,1,0:T(8,128)(2,1)}), bf16[8,8,64,512]{3,2,1,0:T(8,128)(2,1)}, u32[]{:S(2)}, u32[]{:S(2)}) %all-to-all-start.2) | async-done | bytes 4194336 | tf_op jit(solution)/shard_map/all_to_all | solution.py:456
  120.2 6.5 all-to-all-start.1
  131.0 6.5 collective-permute-done.refs_1_
  139.4 12.6 compress.3
  152.0 516.5 %all-to-all-done.1.refs_2_ = bf16[8,8,64,3072]{3,2,1,0:T(8,128)(2,1)} async-done(((bf16[8,8,64,3072]{3,2,1,0:T(8,128)(2,1)}), bf16[8,8,64,3072]{3,2,1,0:T(8,128)(2,1)}, u32[]{:S(2)}, u32[]{:S(2)}) %all-to-all-start.1) | async-done | bytes 25165856 | tf_op jit(solution)/shard_map/all_to_all | solution.py:456
  673.2 8.4 doppler.3
  681.6 35.9 %doppler.4 = (bf16[8,24,16,4096]{3,2,1,0:T(8,128)(2,1)}, bf16[8,6,16,4096]{3,2,1,0:T(8,128)(2,1)}, bf16[8,2,16,4096]{3,2,1,0:T(8,128)(2,1)S(1)}) custom-call(bf16[512,512]{1,0:T(8,128)(2,1)S(1)} %copy-done.1, bf16[512,512]{1,0:T(8,128)(2,1)S(1)} %copy-done.2, ...), custom_call_target="tpu_custom_call", output_to_operand_aliasing={{0}: (3, {}), {1}: (4, {}), {2}: (5, {})} | custom-call | flops 25769803776 | bytes 50331648 | tf_op jit(solution)/shard_map/doppler/pallas_call | solution.py:202
  717.6 48.0 %all-to-all-done.refs_2_ = bf16[8,8,64,512]{3,2,1,0:T(8,128)(2,1)} async-done(((bf16[8,8,64,512]{3,2,1,0:T(8,128)(2,1)}), bf16[8,8,64,512]{3,2,1,0:T(8,128)(2,1)}, u32[]{:S(2)}, u32[]{:S(2)}) %all-to-all-start) | async-done | bytes 4194336 | tf_op jit(solution)/shard_map/all_to_all | solution.py:456
  765.6 8.4 doppler.5
  774.0 550.3 %all_to_all.30.data_ref = bf16[8,24,16,4096]{3,2,1,0:T(8,128)(2,1)} all-to-all(bf16[8,24,16,4096]{3,2,1,0:T(8,128)(2,1)} %get-tuple-element.27), channel_id=1, replica_groups=mesh['dop'=8,'rng'=4] {'dop'}, dimensions={0} | all-to-all | bytes 50331648 | tf_op jit(solution)/shard_map/all_to_all | solution.py:456
  1329.6 14.5 gram.3
  1344.1 20.9 %all-gather.5.cloned.1.call-done = f32[96,32,128]{2,1,0:T(8,128)} async-done(((f32[24,32,128]{2,1,0:T(8,128)}), f32[96,32,128]{2,1,0:T(8,128)}) %all-gather.5.cloned.1.call-update) | async-done | bytes 1572880 | tf_op jit(solution)/shard_map/all_gather | solution.py:506
  1366.4 26.4 %inverse_factors.3.inverse_ref = bf16[24,256,128]{2,1,0:T(8,128)(2,1)S(1)} custom-call(s32[1]{0:T(128)} %bitcast.segment_ref, s32[24]{0:T(128)S(1)} %bitcast.9, s32[24]{0:T(128)S(1)} %bitcast.11, f32[4,24,32,128]{3,2,1,0:T(8,128)S(1)} %bitcast.10), custom_call_target="tpu_custom_call" | custom-call | flops 2013265920 | bytes 1572864 | tf_op jit(solution)/shard_map/inverse_factors/pallas_call | solution.py:401
  1392.8 23.1 %whiten.3.refs_0_ = bf16[32,128,4096]{2,1,0:T(8,128)(2,1)} custom-call(bf16[24,256,128]{2,1,0:T(8,128)(2,1)S(1)} %inverse_factors.3.inverse_ref, bf16[8,24,16,4096]{3,2,1,0:T(8,128)(2,1)} %all_to_all.30.data_ref), custom_call_target="tpu_custom_call" | custom-call | flops 6442450944 | bytes 50331648 | tf_op jit(solution)/shard_map/whiten/pallas_call | solution.py:442
  1415.9 50.0 %all-to-all-done.4.data_ref = bf16[8,6,16,4096]{3,2,1,0:T(8,128)(2,1)} async-done(((bf16[8,6,16,4096]{3,2,1,0:T(8,128)(2,1)}), bf16[8,6,16,4096]{3,2,1,0:T(8,128)(2,1)}, u32[]{:S(2)}, u32[]{:S(2)}) %all-to-all-start.4) | async-done | bytes 6291488 | tf_op jit(solution)/shard_map/all_to_all | solution.py:456
  1470.0 5.8 gram.5
  1475.8 6.5 all-gather.2
  1482.3 12.2 inverse_factors.5.inverse_ref
  1494.5 8.1 whiten.4.refs_0_
  1502.6 15.3 all-to-all-done.5.data_ref
  1524.9 8.8 inverse_factors.4.inverse_ref
  (30 shorter events, 32.2 us)
Async XLA Ops:
  19.7 100.5 %all-to-all-start.2 = ((bf16[8,8,64,512]{3,2,1,0:T(8,128)(2,1)}), bf16[8,8,64,512]{3,2,1,0:T(8,128)(2,1)}, u32[]{:S(2)}, u32[]{:S(2)}) async-start(bf16[8,8,64,512]{3,2,1,0:T(8,128)(2,1)} %compress.5), calls=%async_computation.2 | async-start | bytes 8388608 | tf_op jit(solution)/shard_map/all_to_all | solution.py:456
  120.2 548.2 %all-to-all-start.1 = ((bf16[8,8,64,3072]{3,2,1,0:T(8,128)(2,1)}), bf16[8,8,64,3072]{3,2,1,0:T(8,128)(2,1)}, u32[]{:S(2)}, u32[]{:S(2)}) async-start(bf16[8,8,64,3072]{3,2,1,0:T(8,128)(2,1)} %compress.4), calls=%async_computation.1 | async-start | bytes 50331648 | tf_op jit(solution)/shard_map/all_to_all | solution.py:456
  129.4 8.1 collective-permute-start
  137.5 1.9 copy-start.6
  152.0 521.2 %copy-start.1 = (bf16[512,512]{1,0:T(8,128)(2,1)S(1)}, bf16[512,512]{1,0:T(8,128)(2,1)}, u32[]{:S(2)}) copy-start(bf16[512,512]{1,0:T(8,128)(2,1)} %constant.10.clone.refs_0_) | copy-start | bytes 1572868
  152.0 521.2 %copy-start.2 = (bf16[512,512]{1,0:T(8,128)(2,1)S(1)}, bf16[512,512]{1,0:T(8,128)(2,1)}, u32[]{:S(2)}) copy-start(bf16[512,512]{1,0:T(8,128)(2,1)} %constant.11.clone.refs_1_) | copy-start | bytes 1572868
  668.5 97.1 %all-to-all-start = ((bf16[8,8,64,512]{3,2,1,0:T(8,128)(2,1)}), bf16[8,8,64,512]{3,2,1,0:T(8,128)(2,1)}, u32[]{:S(2)}, u32[]{:S(2)}) async-start(bf16[8,8,64,512]{3,2,1,0:T(8,128)(2,1)} %compress.3), calls=%async_computation | async-start | bytes 8388608 | tf_op jit(solution)/shard_map/all_to_all | solution.py:456
  774.0 550.3 %copy-start = (bf16[8,2,16,4096]{3,2,1,0:T(8,128)(2,1)}, bf16[8,2,16,4096]{3,2,1,0:T(8,128)(2,1)S(1)}, u32[]{:S(2)}) copy-start(bf16[8,2,16,4096]{3,2,1,0:T(8,128)(2,1)S(1)} %get-tuple-element.30) | copy-start | bytes 6291460
  1324.3 5.2 copy-start.3
  1324.3 141.5 %all-to-all-start.4 = ((bf16[8,6,16,4096]{3,2,1,0:T(8,128)(2,1)}), bf16[8,6,16,4096]{3,2,1,0:T(8,128)(2,1)}, u32[]{:S(2)}, u32[]{:S(2)}) async-start(bf16[8,6,16,4096]{3,2,1,0:T(8,128)(2,1)} %get-tuple-element.28), calls=%async_computation.4 | async-start | bytes 12582912 | tf_op jit(solution)/shard_map/all_to_all | solution.py:456
  1329.3 35.7 %all-gather.5.cloned.1.call-start = ((), (), s32[]{:S(2)}) async-start(), calls=%async_computation.6 | async-start | bytes 1966080 | tf_op jit(solution)/shard_map/all_gather | solution.py:506
  1329.6 35.4 %copy-start.5 = (s32[32]{0:T(128)S(1)}, s32[32]{0:T(128)}, u32[]{:S(2)}) copy-start(s32[32]{0:T(128)} %param.8) | copy-start | bytes 388
  1365.0 1.4 copy-start.4
  1465.9 52.1 %all-to-all-start.5 = ((bf16[8,2,16,4096]{3,2,1,0:T(8,128)(2,1)}), bf16[8,2,16,4096]{3,2,1,0:T(8,128)(2,1)S(1)}, u32[]{:S(2)}, u32[]{:S(2)}) async-start(bf16[8,2,16,4096]{3,2,1,0:T(8,128)(2,1)} %copy-done), calls=%async_computation.5 | async-start | bytes 4194304 | tf_op jit(solution)/shard_map/all_to_all | solution.py:456
Sparse Core Ops, SparseCore 0:
  1344.2 20.7 all-gather.4

commit v4 on v3

--- a/solution.py
+++ b/solution.py
@@ -14,6 +14,7 @@
 LANES = 128
 BINS_AT_ONCE = 4
 PANEL = 16
+TILE = 128
 WIDTH = 256
 VMEM_LIMIT = 50 * 1024 * 1024
 
@@ -37,27 +38,27 @@
 
 
 def table_kernel(taps, sequence_ref, table_ref):
-    rows = taps + WIDTH
+    rows = taps + TILE
     length = sequence_ref.shape[1]
     tables = []
     for component in range(2):
         wide = jnp.broadcast_to(sequence_ref[component : component + 1, :], (rows, length))
         rolled = pltpu.roll(wide, 0, 1, stride=1, stride_axis=0)
-        tables.append(rolled[:, :WIDTH])
+        tables.append(rolled[:, :TILE])
     real, imag = tables
-    table_ref[:rows, :WIDTH] = real.astype(table_ref.dtype)
-    table_ref[:rows, WIDTH:] = imag.astype(table_ref.dtype)
-    table_ref[rows:, :WIDTH] = (-imag).astype(table_ref.dtype)
-    table_ref[rows:, WIDTH:] = real.astype(table_ref.dtype)
+    table_ref[:rows, :TILE] = real.astype(table_ref.dtype)
+    table_ref[:rows, TILE:] = imag.astype(table_ref.dtype)
+    table_ref[rows:, :TILE] = (-imag).astype(table_ref.dtype)
+    table_ref[rows:, TILE:] = real.astype(table_ref.dtype)
 
 
 def filter_table(chirp):
     taps = chirp.shape[1]
-    pad = taps + WIDTH - taps % WIDTH - WIDTH
+    pad = taps + TILE - taps % TILE - TILE
     sequence = jnp.concatenate([jnp.zeros((2, pad), chirp.dtype), chirp], axis=1).astype(jnp.float32)
     return pl.pallas_call(
         functools.partial(table_kernel, taps),
-        out_shape=jax.ShapeDtypeStruct((2 * (taps + WIDTH), 2 * WIDTH), chirp.dtype),
+        out_shape=jax.ShapeDtypeStruct((2 * (taps + TILE), 2 * TILE), chirp.dtype),
         compiler_params=params(),
         name="filter_table",
     )(sequence)
@@ -65,9 +66,9 @@
 
 def compress_kernel(taps, has_halo, group, *refs):
     if has_halo:
-        table_ref, halo_ref, before_ref, now_ref, out_ref, wide_ref = refs
+        table_ref, halo_ref, before_ref, now_ref, out_ref, *slots = refs
     else:
-        table_ref, before_ref, now_ref, out_ref, wide_ref = refs
+        table_ref, before_ref, now_ref, out_ref, *slots = refs
     pulses, channels, gates = now_ref.shape[1:]
     rows = pulses * channels
     parts = []
@@ -80,13 +81,14 @@
                 [before.reshape(rows, taps), now_ref[component].reshape(rows, gates)], axis=1
             )
         )
-    for tile in range(gates // WIDTH):
-        first = tile * WIDTH
-        window = jnp.concatenate([part[:, first : first + taps + WIDTH] for part in parts], axis=1)
+    for tile in range(gates // TILE):
+        first = tile * TILE
+        wide_ref = slots[tile % len(slots)]
+        window = jnp.concatenate([part[:, first : first + taps + TILE] for part in parts], axis=1)
         filtered = jnp.dot(window, table_ref[...], preferred_element_type=jnp.float32)
-        per_part = WIDTH // LANES
+        per_part = TILE // LANES
         for lane_tile in range(2 * per_part):
-            wide_ref[lane_tile] = filtered[:, lane_tile * LANES : (lane_tile + 1) * LANES]
+            wide_ref[lane_tile, :rows] = filtered[:, lane_tile * LANES : (lane_tile + 1) * LANES]
         for channel in range(channels):
             for lane_tile in range(2 * per_part):
                 component = lane_tile // per_part
@@ -102,7 +104,7 @@
 
 def compress(echoes, table, halo, start, size, groups):
     _, pulses, channels, gates = echoes.shape
-    taps = table.shape[0] // 2 - WIDTH
+    taps = table.shape[0] // 2 - TILE
     group = channels // groups
     at_once = max(16, group)
     step = taps
@@ -125,10 +127,13 @@
             (at_once // group, group, 2 * pulses, step), lambda c, g: (c, 0, 0, g)
         ),
         out_shape=jax.ShapeDtypeStruct((groups, group, 2 * pulses, size), echoes.dtype),
-        scratch_shapes=[pltpu.VMEM((2 * WIDTH // LANES, pulses * at_once, LANES), jnp.float32)],
+        scratch_shapes=[
+            pltpu.VMEM((2 * TILE // LANES, (pulses + 1) * at_once, LANES), jnp.float32)
+        ]
+        * 2,
         compiler_params=params(),
         cost_estimate=cost(
-            2 * pulses * channels * size * (taps + WIDTH) * 4, 12 * pulses * channels * size
+            2 * pulses * channels * size * (taps + TILE) * 4, 12 * pulses * channels * size
         ),
         name="compress",
     )(*operands)
@@ -211,7 +216,7 @@
             jax.ShapeDtypeStruct((groups, count, 2 * group, gates), received.dtype)
             for _, count in plan
         ],
-        scratch_shapes=[pltpu.VMEM((step // LANES, group * total, LANES), jnp.float32)],
+        scratch_shapes=[pltpu.VMEM((step // LANES, group * (total + 1), LANES), jnp.float32)],
         input_output_aliases=aliases,
         compiler_params=params(),
         cost_estimate=cost(4 * total * total * group * size, 4 * total * group * size),

time: 1540 us -> 1540 us (level)
  no operation moved by 1% of the time
where the time goes in v4:
time: 1540 us
  waiting for transfers between devices  697 us (45%)
  blocking collectives  562 us (36%)
  Pallas kernels  233 us (15%)
  starting transfers between devices  29.1 us (2%)
    all_to_all x5, waiting for transfers between devices, exchange(): return lax.all_to_all(array, 'dop', split_axis=0, concat_axis=0, tiled=True)  670 us
    all_to_all x1, blocking collectives, exchange(): return lax.all_to_all(array, 'dop', split_axis=0, concat_axis=0, tiled=True)  550 us
    pallas_call x3, Pallas kernels, compress(): pl.pallas_call(functools.partial(compress_kernel, taps, has_halo, group),...  76.8 us
    pallas_call x3, Pallas kernels, doppler(): pl.pallas_call(functools.partial(doppler_kernel, plan, 0 if earlier is No...  52.7 us
    pallas_call x3, Pallas kernels, inverse_factors(): pl.pallas_call(functools.partial(factor_kernel, groups), in_specs=[smem,...  47.3 us
    pallas_call x3, Pallas kernels, whiten(): pl.pallas_call(whiten_kernel, grid=(bins // at_once,), in_specs=in_specs,...  33.8 us
  transfers between devices with their start and end apart: 7, of which 7 were waited for; matrix products, arithmetic and copies ran while one was open for 0% of the time, Pallas kernels for 13%

profile of v4, /device:TPU:0, one launch (start us, length us, event | category | flops | bytes accessed | tf_op | source)
XLA Modules:
  0.0 1541.8 jit_solution(6042722856993038207)
XLA Ops:
  7.4 11.1 compress.5
  18.5 7.3 all-to-all-start.2
  25.8 54.2 %compress.4 = bf16[8,8,64,3072]{3,2,1,0:T(8,128)(2,1)} custom-call(bf16[1280,256]{1,0:T(8,128)(2,1)S(1)} %filter_table.1.refs_0_, bf16[2,32,64,4096]{3,2,1,0:T(8,128)(2,1)} %refs_2_.5, bf16[2,32,64,4096]{3,2,1,0:T(8,128)(2,1)} %refs_2_.5), custom_call_target="tpu_custom_call" | custom-call | flops 32212254720 | bytes 75497472 | tf_op jit(solution)/shard_map/compress/pallas_call | solution.py:122
  80.0 39.1 %all-to-all-done.2.refs_2_ = bf16[8,8,64,512]{3,2,1,0:T(8,128)(2,1)} async-done(((bf16[8,8,64,512]{3,2,1,0:T(8,128)(2,1)}), bf16[8,8,64,512]{3,2,1,0:T(8,128)(2,1)}, u32[]{:S(2)}, u32[]{:S(2)}) %all-to-all-start.2) | async-done | bytes 4194336 | tf_op jit(solution)/shard_map/all_to_all | solution.py:461
  119.0 6.5 all-to-all-start.1
  129.8 6.5 collective-permute-done.refs_1_
  138.2 11.5 compress.3
  149.8 517.5 %all-to-all-done.1.refs_2_ = bf16[8,8,64,3072]{3,2,1,0:T(8,128)(2,1)} async-done(((bf16[8,8,64,3072]{3,2,1,0:T(8,128)(2,1)}), bf16[8,8,64,3072]{3,2,1,0:T(8,128)(2,1)}, u32[]{:S(2)}, u32[]{:S(2)}) %all-to-all-start.1) | async-done | bytes 25165856 | tf_op jit(solution)/shard_map/all_to_all | solution.py:461
  672.0 8.4 doppler.3
  680.4 36.0 %doppler.4 = (bf16[8,24,16,4096]{3,2,1,0:T(8,128)(2,1)}, bf16[8,6,16,4096]{3,2,1,0:T(8,128)(2,1)}, bf16[8,2,16,4096]{3,2,1,0:T(8,128)(2,1)S(1)}) custom-call(bf16[512,512]{1,0:T(8,128)(2,1)S(1)} %copy-done.1, bf16[512,512]{1,0:T(8,128)(2,1)S(1)} %copy-done.2, ...), custom_call_target="tpu_custom_call", output_to_operand_aliasing={{0}: (3, {}), {1}: (4, {}), {2}: (5, {})} | custom-call | flops 25769803776 | bytes 50331648 | tf_op jit(solution)/shard_map/doppler/pallas_call | solution.py:207
  716.4 48.0 %all-to-all-done.refs_2_ = bf16[8,8,64,512]{3,2,1,0:T(8,128)(2,1)} async-done(((bf16[8,8,64,512]{3,2,1,0:T(8,128)(2,1)}), bf16[8,8,64,512]{3,2,1,0:T(8,128)(2,1)}, u32[]{:S(2)}, u32[]{:S(2)}) %all-to-all-start) | async-done | bytes 4194336 | tf_op jit(solution)/shard_map/all_to_all | solution.py:461
  764.4 8.4 doppler.5
  772.8 550.3 %all_to_all.30.data_ref = bf16[8,24,16,4096]{3,2,1,0:T(8,128)(2,1)} all-to-all(bf16[8,24,16,4096]{3,2,1,0:T(8,128)(2,1)} %get-tuple-element.27), channel_id=1, replica_groups=mesh['dop'=8,'rng'=4] {'dop'}, dimensions={0} | all-to-all | bytes 50331648 | tf_op jit(solution)/shard_map/all_to_all | solution.py:461
  1328.4 14.5 gram.3
  1342.9 20.9 %all-gather.5.cloned.1.call-done = f32[96,32,128]{2,1,0:T(8,128)} async-done(((f32[24,32,128]{2,1,0:T(8,128)}), f32[96,32,128]{2,1,0:T(8,128)}) %all-gather.5.cloned.1.call-update) | async-done | bytes 1572880 | tf_op jit(solution)/shard_map/all_gather | solution.py:511
  1365.2 26.3 %inverse_factors.3.inverse_ref = bf16[24,256,128]{2,1,0:T(8,128)(2,1)S(1)} custom-call(s32[1]{0:T(128)} %bitcast.segment_ref, s32[24]{0:T(128)S(1)} %bitcast.9, s32[24]{0:T(128)S(1)} %bitcast.11, f32[4,24,32,128]{3,2,1,0:T(8,128)S(1)} %bitcast.10), custom_call_target="tpu_custom_call" | custom-call | flops 2013265920 | bytes 1572864 | tf_op jit(solution)/shard_map/inverse_factors/pallas_call | solution.py:406
  1391.6 23.1 %whiten.3.refs_0_ = bf16[32,128,4096]{2,1,0:T(8,128)(2,1)} custom-call(bf16[24,256,128]{2,1,0:T(8,128)(2,1)S(1)} %inverse_factors.3.inverse_ref, bf16[8,24,16,4096]{3,2,1,0:T(8,128)(2,1)} %all_to_all.30.data_ref), custom_call_target="tpu_custom_call" | custom-call | flops 6442450944 | bytes 50331648 | tf_op jit(solution)/shard_map/whiten/pallas_call | solution.py:447
  1414.7 49.9 %all-to-all-done.4.data_ref = bf16[8,6,16,4096]{3,2,1,0:T(8,128)(2,1)} async-done(((bf16[8,6,16,4096]{3,2,1,0:T(8,128)(2,1)}), bf16[8,6,16,4096]{3,2,1,0:T(8,128)(2,1)}, u32[]{:S(2)}, u32[]{:S(2)}) %all-to-all-start.4) | async-done | bytes 6291488 | tf_op jit(solution)/shard_map/all_to_all | solution.py:461
  1468.8 5.8 gram.5
  1474.6 6.5 all-gather.2
  1481.0 12.2 inverse_factors.5.inverse_ref
  1493.3 8.1 whiten.4.refs_0_
  1501.4 15.3 all-to-all-done.5.data_ref
  1523.6 8.8 inverse_factors.4.inverse_ref
  (30 shorter events, 32.1 us)
Async XLA Ops:
  18.5 100.5 %all-to-all-start.2 = ((bf16[8,8,64,512]{3,2,1,0:T(8,128)(2,1)}), bf16[8,8,64,512]{3,2,1,0:T(8,128)(2,1)}, u32[]{:S(2)}, u32[]{:S(2)}) async-start(bf16[8,8,64,512]{3,2,1,0:T(8,128)(2,1)} %compress.5), calls=%async_computation.2 | async-start | bytes 8388608 | tf_op jit(solution)/shard_map/all_to_all | solution.py:461
  119.0 548.2 %all-to-all-start.1 = ((bf16[8,8,64,3072]{3,2,1,0:T(8,128)(2,1)}), bf16[8,8,64,3072]{3,2,1,0:T(8,128)(2,1)}, u32[]{:S(2)}, u32[]{:S(2)}) async-start(bf16[8,8,64,3072]{3,2,1,0:T(8,128)(2,1)} %compress.4), calls=%async_computation.1 | async-start | bytes 50331648 | tf_op jit(solution)/shard_map/all_to_all | solution.py:461
  128.2 8.1 collective-permute-start
  136.3 1.9 copy-start.6
  149.8 522.2 %copy-start.1 = (bf16[512,512]{1,0:T(8,128)(2,1)S(1)}, bf16[512,512]{1,0:T(8,128)(2,1)}, u32[]{:S(2)}) copy-start(bf16[512,512]{1,0:T(8,128)(2,1)} %constant.10.clone.refs_0_) | copy-start | bytes 1572868
  149.8 522.3 %copy-start.2 = (bf16[512,512]{1,0:T(8,128)(2,1)S(1)}, bf16[512,512]{1,0:T(8,128)(2,1)}, u32[]{:S(2)}) copy-start(bf16[512,512]{1,0:T(8,128)(2,1)} %constant.11.clone.refs_1_) | copy-start | bytes 1572868
  667.3 97.1 %all-to-all-start = ((bf16[8,8,64,512]{3,2,1,0:T(8,128)(2,1)}), bf16[8,8,64,512]{3,2,1,0:T(8,128)(2,1)}, u32[]{:S(2)}, u32[]{:S(2)}) async-start(bf16[8,8,64,512]{3,2,1,0:T(8,128)(2,1)} %compress.3), calls=%async_computation | async-start | bytes 8388608 | tf_op jit(solution)/shard_map/all_to_all | solution.py:461
  772.8 550.3 %copy-start = (bf16[8,2,16,4096]{3,2,1,0:T(8,128)(2,1)}, bf16[8,2,16,4096]{3,2,1,0:T(8,128)(2,1)S(1)}, u32[]{:S(2)}) copy-start(bf16[8,2,16,4096]{3,2,1,0:T(8,128)(2,1)S(1)} %get-tuple-element.30) | copy-start | bytes 6291460
  1323.1 5.2 copy-start.3
  1323.1 141.5 %all-to-all-start.4 = ((bf16[8,6,16,4096]{3,2,1,0:T(8,128)(2,1)}), bf16[8,6,16,4096]{3,2,1,0:T(8,128)(2,1)}, u32[]{:S(2)}, u32[]{:S(2)}) async-start(bf16[8,6,16,4096]{3,2,1,0:T(8,128)(2,1)} %get-tuple-element.28), calls=%async_computation.4 | async-start | bytes 12582912 | tf_op jit(solution)/shard_map/all_to_all | solution.py:461
  1328.1 35.7 %all-gather.5.cloned.1.call-start = ((), (), s32[]{:S(2)}) async-start(), calls=%async_computation.6 | async-start | bytes 1966080 | tf_op jit(solution)/shard_map/all_gather | solution.py:511
  1328.4 35.4 %copy-start.5 = (s32[32]{0:T(128)S(1)}, s32[32]{0:T(128)}, u32[]{:S(2)}) copy-start(s32[32]{0:T(128)} %param.8) | copy-start | bytes 388
  1363.8 1.4 copy-start.4
  1464.6 52.1 %all-to-all-start.5 = ((bf16[8,2,16,4096]{3,2,1,0:T(8,128)(2,1)}), bf16[8,2,16,4096]{3,2,1,0:T(8,128)(2,1)S(1)}, u32[]{:S(2)}, u32[]{:S(2)}) async-start(bf16[8,2,16,4096]{3,2,1,0:T(8,128)(2,1)} %copy-done), calls=%async_computation.5 | async-start | bytes 4194304 | tf_op jit(solution)/shard_map/all_to_all | solution.py:461
Sparse Core Ops, SparseCore 0:
  1343.0 20.7 all-gather.4

commit v5 on v4

--- a/solution.py
+++ b/solution.py
@@ -400,59 +400,60 @@
         out_ref[b, size:, :] = (inverse - high.astype(jnp.float32)).astype(jnp.bfloat16)
 
 
-def inverse_factors(grams, segment, counts, ridge, groups):
-    segments, bins, quarter, size = grams.shape
-    smem = pl.BlockSpec(memory_space=pltpu.SMEM)
-    return pl.pallas_call(
-        functools.partial(factor_kernel, groups),
-        in_specs=[smem, smem, smem, pl.BlockSpec(memory_space=pltpu.VMEM)],
-        out_specs=pl.BlockSpec(memory_space=pltpu.VMEM),
-        out_shape=jax.ShapeDtypeStruct((bins, 2 * size, size), jnp.bfloat16),
-        scratch_shapes=[
-            pltpu.VMEM((bins, size, size), jnp.float32),
-            pltpu.VMEM((bins, size, size), jnp.float32),
-        ],
-        compiler_params=params(),
-        cost_estimate=cost(2 * bins * size**3 * 20, 4 * segments * bins * quarter * size),
-        name="inverse_factors",
-    )(segment, counts, ridge, grams)
-
-
-def whiten_kernel(inverse_ref, data_ref, *refs):
-    out_ref = refs[-1]
+def whiten_kernel(segment_ref, counts_ref, ridge_ref, grams_ref, data_ref, *refs):
+    out_ref, work_ref, inverse_ref, solved_ref = refs[-4:]
     groups, bins, rows, gates = data_ref.shape
     size = groups * rows
+
+    @pl.when(pl.program_id(0) == 0)
+    def _():
+        factor_kernel(
+            groups, segment_ref, counts_ref, ridge_ref, grams_ref, solved_ref, work_ref, inverse_ref
+        )
+
     step = 1024 if gates % 1024 == 0 else gates
     for b in range(bins):
+        inverse = solved_ref[pl.program_id(0) * bins + b]
         for first in range(0, gates, step):
             data = data_ref[:, b, :, first : first + step].reshape(size, step)
-            both = jnp.dot(inverse_ref[b], data, preferred_element_type=jnp.float32)
+            both = jnp.dot(inverse, data, preferred_element_type=jnp.float32)
             out_ref[b, :, first : first + step] = (both[:size] + both[size:]).astype(out_ref.dtype)
 
 
-def whiten(inverse, data, earlier, first, total):
+def whiten(grams, segment, counts, ridge, data, earlier, first, total):
     groups, bins, rows, gates = data.shape
     size = groups * rows
     at_once = next(k for k in (BINS_AT_ONCE, 2, 1) if bins % k == 0 and first % k == 0)
+    smem = pl.BlockSpec(memory_space=pltpu.SMEM)
     in_specs = [
-        pl.BlockSpec((at_once, 2 * size, size), lambda b: (b, 0, 0)),
+        smem,
+        smem,
+        smem,
+        pl.BlockSpec(grams.shape, lambda b: (0, 0, 0, 0)),
         pl.BlockSpec((groups, at_once, rows, gates), lambda b: (0, b, 0, 0)),
     ]
-    operands = [inverse, data]
+    operands = [segment, counts, ridge, grams, data]
     aliases = {}
     if earlier is not None:
         in_specs.append(pl.BlockSpec(memory_space=pl.ANY))
         operands.append(earlier)
-        aliases = {2: 0}
+        aliases = {5: 0}
     return pl.pallas_call(
         whiten_kernel,
         grid=(bins // at_once,),
         in_specs=in_specs,
         out_specs=pl.BlockSpec((at_once, size, gates), lambda b: (first // at_once + b, 0, 0)),
         out_shape=jax.ShapeDtypeStruct((total, size, gates), data.dtype),
+        scratch_shapes=[
+            pltpu.VMEM((bins, size, size), jnp.float32),
+            pltpu.VMEM((bins, size, size), jnp.float32),
+            pltpu.VMEM((bins, 2 * size, size), jnp.bfloat16),
+        ],
         input_output_aliases=aliases,
         compiler_params=params(),
-        cost_estimate=cost(4 * bins * size * size * gates, 4 * bins * size * gates),
+        cost_estimate=cost(
+            4 * bins * size * size * gates + 40 * bins * size**3, 4 * bins * size * gates
+        ),
         name="whiten",
     )(*operands)
 
@@ -509,10 +510,9 @@
             data = data.reshape(1, count, 2 * channels, gates)
         these = counts[first : first + count]
         grams = lax.all_gather(gram(data, these), "rng")
-        inverse = inverse_factors(
-            grams, segment, these, ridge[first : first + count], data.shape[0]
+        whitened = whiten(
+            grams, segment, these, ridge[first : first + count], data, whitened, first, bins
         )
-        whitened = whiten(inverse, data, whitened, first, bins)
         data = following
     return whitened
 

time: 1540 us -> 1540 us (level)
    pallas_call x3 -> x0, Pallas kernels: 47.3 us -> none  [inverse_factors(): pl.pallas_call(functools.partial(factor_kernel, groups), in_specs=[smem,...]
    pallas_call x3, Pallas kernels: 33.8 us -> 79.9 us  [whiten(): pl.pallas_call(whiten_kernel, grid=(bins // at_once,), in_specs=in_specs,...]
where the time goes in v5:
time: 1540 us
  waiting for transfers between devices  698 us (45%)
  blocking collectives  562 us (36%)
  Pallas kernels  232 us (15%)
  starting transfers between devices  29.1 us (2%)
    all_to_all x5, waiting for transfers between devices, exchange(): return lax.all_to_all(array, 'dop', split_axis=0, concat_axis=0, tiled=True)  671 us
    all_to_all x1, blocking collectives, exchange(): return lax.all_to_all(array, 'dop', split_axis=0, concat_axis=0, tiled=True)  550 us
    pallas_call x3, Pallas kernels, whiten(): pl.pallas_call(whiten_kernel, grid=(bins // at_once,), in_specs=in_specs,...  79.9 us
    pallas_call x3, Pallas kernels, compress(): pl.pallas_call(functools.partial(compress_kernel, taps, has_halo, group),...  76.8 us
    pallas_call x3, Pallas kernels, doppler(): pl.pallas_call(functools.partial(doppler_kernel, plan, 0 if earlier is No...  52.7 us
  transfers between devices with their start and end apart: 7, of which 7 were waited for; matrix products, arithmetic and copies ran while one was open for 0% of the time, Pallas kernels for 13%

profile of v5, /device:TPU:0, one launch (start us, length us, event | category | flops | bytes accessed | tf_op | source)
XLA Modules:
  0.0 1541.8 jit_solution(13800263422715562843)
XLA Ops:
  7.4 11.1 compress.5
  18.5 7.3 all-to-all-start.2
  25.8 54.2 %compress.4 = bf16[8,8,64,3072]{3,2,1,0:T(8,128)(2,1)} custom-call(bf16[1280,256]{1,0:T(8,128)(2,1)S(1)} %filter_table.1.refs_0_, bf16[2,32,64,4096]{3,2,1,0:T(8,128)(2,1)} %refs_2_.5, bf16[2,32,64,4096]{3,2,1,0:T(8,128)(2,1)} %refs_2_.5), custom_call_target="tpu_custom_call" | custom-call | flops 32212254720 | bytes 75497472 | tf_op jit(solution)/shard_map/compress/pallas_call | solution.py:122
  80.0 39.1 %all-to-all-done.2.refs_2_ = bf16[8,8,64,512]{3,2,1,0:T(8,128)(2,1)} async-done(((bf16[8,8,64,512]{3,2,1,0:T(8,128)(2,1)}), bf16[8,8,64,512]{3,2,1,0:T(8,128)(2,1)}, u32[]{:S(2)}, u32[]{:S(2)}) %all-to-all-start.2) | async-done | bytes 4194336 | tf_op jit(solution)/shard_map/all_to_all | solution.py:462
  119.0 6.5 all-to-all-start.1
  129.8 6.5 collective-permute-done.refs_1_
  138.2 11.5 compress.3
  149.8 517.5 %all-to-all-done.1.refs_2_ = bf16[8,8,64,3072]{3,2,1,0:T(8,128)(2,1)} async-done(((bf16[8,8,64,3072]{3,2,1,0:T(8,128)(2,1)}), bf16[8,8,64,3072]{3,2,1,0:T(8,128)(2,1)}, u32[]{:S(2)}, u32[]{:S(2)}) %all-to-all-start.1) | async-done | bytes 25165856 | tf_op jit(solution)/shard_map/all_to_all | solution.py:462
  672.0 8.4 doppler.3
  680.4 36.0 %doppler.4 = (bf16[8,24,16,4096]{3,2,1,0:T(8,128)(2,1)}, bf16[8,6,16,4096]{3,2,1,0:T(8,128)(2,1)}, bf16[8,2,16,4096]{3,2,1,0:T(8,128)(2,1)S(1)}) custom-call(bf16[512,512]{1,0:T(8,128)(2,1)S(1)} %copy-done.2, bf16[512,512]{1,0:T(8,128)(2,1)S(1)} %copy-done.3, ...), custom_call_target="tpu_custom_call", output_to_operand_aliasing={{0}: (3, {}), {1}: (4, {}), {2}: (5, {})} | custom-call | flops 25769803776 | bytes 50331648 | tf_op jit(solution)/shard_map/doppler/pallas_call | solution.py:207
  716.4 48.0 %all-to-all-done.refs_2_ = bf16[8,8,64,512]{3,2,1,0:T(8,128)(2,1)} async-done(((bf16[8,8,64,512]{3,2,1,0:T(8,128)(2,1)}), bf16[8,8,64,512]{3,2,1,0:T(8,128)(2,1)}, u32[]{:S(2)}, u32[]{:S(2)}) %all-to-all-start) | async-done | bytes 4194336 | tf_op jit(solution)/shard_map/all_to_all | solution.py:462
  764.4 8.4 doppler.5
  772.8 550.3 %all_to_all.30.data_ref = bf16[8,24,16,4096]{3,2,1,0:T(8,128)(2,1)} all-to-all(bf16[8,24,16,4096]{3,2,1,0:T(8,128)(2,1)} %get-tuple-element.27), channel_id=1, replica_groups=mesh['dop'=8,'rng'=4] {'dop'}, dimensions={0} | all-to-all | bytes 50331648 | tf_op jit(solution)/shard_map/all_to_all | solution.py:462
  1323.1 5.0 all-to-all-start.4
  1328.4 14.5 gram.3
  1342.9 20.9 %all-gather.5.cloned.1.call-done = f32[96,32,128]{2,1,0:T(8,128)} async-done(((f32[24,32,128]{2,1,0:T(8,128)}), f32[96,32,128]{2,1,0:T(8,128)}) %all-gather.5.cloned.1.call-update) | async-done | bytes 1572880 | tf_op jit(solution)/shard_map/all_gather | solution.py:512
  1365.2 48.9 %whiten.3.refs_0_ = bf16[32,128,4096]{2,1,0:T(8,128)(2,1)} custom-call(s32[1]{0:T(128)} %bitcast.segment_ref, s32[24]{0:T(128)S(1)} %bitcast.10, s32[24]{0:T(128)S(1)} %bitcast.11, f32[4,24,32,128]{3,2,1,0:T(8,128)S(1)} %bitcast.7, bf16[8,24,16,4096]{3,2,1,0:T(8,128)(2,1)} %all_to_all.30.data_ref), custom_call_target="tpu_custom_call" | custom-call | flops 8455716864 | bytes 50331648 | tf_op jit(solution)/shard_map/whiten/pallas_call | solution.py:441
  1414.1 50.5 %all-to-all-done.4.data_ref = bf16[8,6,16,4096]{3,2,1,0:T(8,128)(2,1)} async-done(((bf16[8,6,16,4096]{3,2,1,0:T(8,128)(2,1)}), bf16[8,6,16,4096]{3,2,1,0:T(8,128)(2,1)}, u32[]{:S(2)}, u32[]{:S(2)}) %all-to-all-start.4) | async-done | bytes 6291488 | tf_op jit(solution)/shard_map/all_to_all | solution.py:462
  1468.8 5.8 gram.5
  1474.6 6.5 all-gather.2
  1481.0 19.8 %whiten.4.refs_0_ = bf16[32,128,4096]{2,1,0:T(8,128)(2,1)} custom-call(s32[1]{0:T(128)} %bitcast.segment_ref, s32[6]{0:T(128)S(1)} %slice.26.counts_ref, s32[6]{0:T(128)S(1)} %slice.27.ridge_ref, f32[4,6,32,128]{3,2,1,0:T(8,128)S(1)} %bitcast.6, bf16[8,6,16,4096]{3,2,1,0:T(8,128)(2,1)} %all-to-all-done.4.data_ref, ...), custom_call_target="tpu_custom_call", output_to_operand_aliasing={{}: (5, {})} | custom-call | flops 2113929216 | bytes 12582912 | tf_op jit(solution)/shard_map/whiten/pallas_call | solution.py:441
  1500.8 15.9 %all-to-all-done.5.data_ref = bf16[8,2,16,4096]{3,2,1,0:T(8,128)(2,1)S(1)} async-done(((bf16[8,2,16,4096]{3,2,1,0:T(8,128)(2,1)}), bf16[8,2,16,4096]{3,2,1,0:T(8,128)(2,1)S(1)}, u32[]{:S(2)}, u32[]{:S(2)}) %all-to-all-start.5) | async-done | bytes 2097184 | tf_op jit(solution)/shard_map/all_to_all | solution.py:462
  1518.2 5.4 all-gather.1
  1523.6 11.3 whiten.5
  (27 shorter events, 19.2 us)
Async XLA Ops:
  18.5 100.5 %all-to-all-start.2 = ((bf16[8,8,64,512]{3,2,1,0:T(8,128)(2,1)}), bf16[8,8,64,512]{3,2,1,0:T(8,128)(2,1)}, u32[]{:S(2)}, u32[]{:S(2)}) async-start(bf16[8,8,64,512]{3,2,1,0:T(8,128)(2,1)} %compress.5), calls=%async_computation.2 | async-start | bytes 8388608 | tf_op jit(solution)/shard_map/all_to_all | solution.py:462
  119.0 548.2 %all-to-all-start.1 = ((bf16[8,8,64,3072]{3,2,1,0:T(8,128)(2,1)}), bf16[8,8,64,3072]{3,2,1,0:T(8,128)(2,1)}, u32[]{:S(2)}, u32[]{:S(2)}) async-start(bf16[8,8,64,3072]{3,2,1,0:T(8,128)(2,1)} %compress.4), calls=%async_computation.1 | async-start | bytes 50331648 | tf_op jit(solution)/shard_map/all_to_all | solution.py:462
  128.2 8.1 collective-permute-start
  136.3 1.9 copy-start.6
  149.8 522.2 %copy-start.2 = (bf16[512,512]{1,0:T(8,128)(2,1)S(1)}, bf16[512,512]{1,0:T(8,128)(2,1)}, u32[]{:S(2)}) copy-start(bf16[512,512]{1,0:T(8,128)(2,1)} %constant.10.clone.refs_0_) | copy-start | bytes 1572868
  149.8 522.3 %copy-start.3 = (bf16[512,512]{1,0:T(8,128)(2,1)S(1)}, bf16[512,512]{1,0:T(8,128)(2,1)}, u32[]{:S(2)}) copy-start(bf16[512,512]{1,0:T(8,128)(2,1)} %constant.11.clone.refs_1_) | copy-start | bytes 1572868
  667.3 97.1 %all-to-all-start = ((bf16[8,8,64,512]{3,2,1,0:T(8,128)(2,1)}), bf16[8,8,64,512]{3,2,1,0:T(8,128)(2,1)}, u32[]{:S(2)}, u32[]{:S(2)}) async-start(bf16[8,8,64,512]{3,2,1,0:T(8,128)(2,1)} %compress.3), calls=%async_computation | async-start | bytes 8388608 | tf_op jit(solution)/shard_map/all_to_all | solution.py:462
  772.8 550.3 %copy-start = (bf16[8,2,16,4096]{3,2,1,0:T(8,128)(2,1)}, bf16[8,2,16,4096]{3,2,1,0:T(8,128)(2,1)S(1)}, u32[]{:S(2)}) copy-start(bf16[8,2,16,4096]{3,2,1,0:T(8,128)(2,1)S(1)} %get-tuple-element.30) | copy-start | bytes 6291460
  1323.1 5.2 copy-start.4
  1323.1 141.5 %all-to-all-start.4 = ((bf16[8,6,16,4096]{3,2,1,0:T(8,128)(2,1)}), bf16[8,6,16,4096]{3,2,1,0:T(8,128)(2,1)}, u32[]{:S(2)}, u32[]{:S(2)}) async-start(bf16[8,6,16,4096]{3,2,1,0:T(8,128)(2,1)} %get-tuple-element.28), calls=%async_computation.4 | async-start | bytes 12582912 | tf_op jit(solution)/shard_map/all_to_all | solution.py:462
  1328.1 35.7 %all-gather.5.cloned.1.call-start = ((), (), s32[]{:S(2)}) async-start(), calls=%async_computation.6 | async-start | bytes 1966080 | tf_op jit(solution)/shard_map/all_gather | solution.py:512
  1328.4 35.4 %copy-start.5 = (s32[32]{0:T(128)S(1)}, s32[32]{0:T(128)}, u32[]{:S(2)}) copy-start(s32[32]{0:T(128)} %param.8) | copy-start | bytes 388
  1363.8 1.4 copy-start.1
  1464.6 52.1 %all-to-all-start.5 = ((bf16[8,2,16,4096]{3,2,1,0:T(8,128)(2,1)}), bf16[8,2,16,4096]{3,2,1,0:T(8,128)(2,1)S(1)}, u32[]{:S(2)}, u32[]{:S(2)}) async-start(bf16[8,2,16,4096]{3,2,1,0:T(8,128)(2,1)} %copy-done), calls=%async_computation.5 | async-start | bytes 4194304 | tf_op jit(solution)/shard_map/all_to_all | solution.py:462
Sparse Core Ops, SparseCore 0:
  1343.0 20.7 all-gather.4
